TPU v7x, 512 devices: a whole 4x4x16 slice. The times are simulated.
512 devices in a mesh: row: 32 (over y, x, z_hi), col: 16 (over z_lo, core).
Axes of the slice: x: 4, y: 4, z: 16 (z_hi: 2, z_lo: 8; z = z_hi * 8 + z_lo), core: 2. Of those that a mesh axis runs over, the one named last changes fastest.
Arguments:
- x_block: float32 [8, 131072], P(None, ('row', 'col')), may hold values from -6 to 6
- p_block: float32 [8, 131072], P(None, ('row', 'col')), may hold values from -6 to 6
- hp_block: float32 [8, 131072], P(None, ('row', 'col')), may hold values from -6 to 6
- tile_rows: int32 [32, 16, 48], P('row', 'col'), may hold values from 0 to 31, as said below
- tile_cols: int32 [32, 16, 48], P('row', 'col'), may hold values from 0 to 63
- tile_count: int32 [32, 16], P('row', 'col'), may hold values from 1 to 48, as said below
- tile_values: bfloat16 [32, 16, 48, 128, 128], P('row', 'col'), may hold values from -0.109375 to 0.109375
Outputs:
- residual: float32 [8, 131072], P(None, ('row', 'col'))
- image: float32 [8, 131072], P(None, ('row', 'col'))
- gram_s: float32 [24, 24], replicated
- gram_h: float32 [24, 24], replicated
Inputs may be any that keep to these rules, and one draw needn't show every extreme that they name: `tile_rows`: together with tile_cols, every live tile lies on or below the diagonal of segments. `tile_count`: every device has at least one live slot; some device has all 48 slots live.
All inputs are finite; a program needn't handle non-finite values.
Results may differ from a plain program's by a relative error of at most 0.007.
Values may be sent and summed in bfloat16 or wider, within the bound.
A program may use at most 64 MiB of HBM per device.

v0:
```python
import jax
import jax.numpy as jnp
from jax import lax
from jax.sharding import PartitionSpec as P


def inner_products(left_rows, right_rows):
    return jnp.dot(
        left_rows, right_rows.T, precision=lax.Precision.HIGHEST, preferred_element_type=jnp.float32
    )


def body(x_block, p_block, hp_block, tile_rows, tile_cols, tile_count, tile_values):
    vectors, seg_width = x_block.shape
    tile_size = tile_values.shape[-1]
    slot_total = tile_values.shape[2]
    row_index = tile_rows.reshape(slot_total)
    col_index = tile_cols.reshape(slot_total)
    stored = tile_values.reshape(slot_total, tile_size, tile_size)
    live_count = tile_count.reshape(())

    def apply_hamiltonian(vector_in):
        rounded = vector_in.astype(jnp.bfloat16)
        column_group = lax.all_gather(rounded, "row", axis=1, tiled=True)
        row_group = lax.all_gather(rounded, "col", axis=1, tiled=True)
        row_segments = row_group.shape[1] // tile_size
        col_segments = column_group.shape[1] // tile_size
        col_blocks = column_group.reshape(vectors, col_segments, tile_size)
        row_blocks = row_group.reshape(vectors, row_segments, tile_size)
        live_mask = (jnp.arange(slot_total, dtype=jnp.int32) < live_count).astype(jnp.float32)
        source_cols = jnp.take(col_blocks, col_index, axis=1)
        source_rows = jnp.take(row_blocks, row_index, axis=1)
        forward = jnp.einsum(
            "vtb,tab->vta", source_cols, stored, preferred_element_type=jnp.float32
        )
        backward = jnp.einsum(
            "vta,tab->vtb", source_rows, stored, preferred_element_type=jnp.float32
        )
        hit_rows = (
            row_index[:, None] == jnp.arange(row_segments, dtype=jnp.int32)[None, :]
        ).astype(jnp.float32) * live_mask[:, None]
        hit_cols = (
            col_index[:, None] == jnp.arange(col_segments, dtype=jnp.int32)[None, :]
        ).astype(jnp.float32) * live_mask[:, None]
        row_part = jnp.einsum("vta,tr->vra", forward, hit_rows)
        col_part = jnp.einsum("vtb,tc->vcb", backward, hit_cols)
        row_part = row_part.reshape(vectors, row_segments * tile_size)
        col_part = col_part.reshape(vectors, col_segments * tile_size)
        row_total = lax.psum(row_part, "col")
        col_total = lax.psum(col_part, "row")
        mine_rows = lax.dynamic_slice_in_dim(
            row_total, lax.axis_index("col") * seg_width, seg_width, 1
        )
        mine_cols = lax.dynamic_slice_in_dim(
            col_total, lax.axis_index("row") * seg_width, seg_width, 1
        )
        return mine_rows + mine_cols

    hx_block = apply_hamiltonian(x_block)
    numerator, denominator = lax.psum(
        (jnp.sum(x_block * hx_block, axis=1), jnp.sum(x_block * x_block, axis=1)), ("row", "col")
    )
    theta = numerator / denominator
    residual = hx_block - theta[:, None] * x_block
    stacked = jnp.concatenate([x_block, residual, p_block], axis=0)
    total_cells = seg_width * lax.axis_size("row") * lax.axis_size("col")
    image = apply_hamiltonian(residual)
    images = jnp.concatenate([hx_block, image, hp_block], axis=0)
    gram_s, gram_h = lax.psum(
        (inner_products(stacked, stacked), inner_products(stacked, images)), ("row", "col")
    )
    return (residual, image, gram_s / total_cells, gram_h / total_cells)


def solution(mesh):
    in_specs = (
        P(None, ("row", "col")),
        P(None, ("row", "col")),
        P(None, ("row", "col")),
        P("row", "col", None),
        P("row", "col", None),
        P("row", "col"),
        P("row", "col", None, None, None),
    )
    out_specs = (P(None, ("row", "col")), P(None, ("row", "col")), P(), P())
    return jax.shard_map(body, mesh=mesh, in_specs=in_specs, out_specs=out_specs, check_vma=False)
```

profile of v0, /device:TPU:1, one launch (start us, length us, event | category | flops | bytes accessed | tf_op | source)
XLA Modules:
  0.0 2101.6 jit_solution(17136051874751186220)
XLA Ops:
  7.2 0.0 copy-start
  7.2 0.0 copy-start.6
  7.2 0.0 all-reduce.7.cloned.1.call-start
  7.2 0.8 compare_select_fusion.1
  8.0 0.7 compare_and_fusion.1
  8.7 0.7 convert_element_type.19
  10.0 151.1 %all_gather.12 = bf16[8,8192]{1,0:T(8,128)(2,1)S(1)} all-gather(bf16[8,256]{1,0:T(8,128)(2,1)S(1)} %convert_element_type.19), channel_id=1, replica_groups=mesh['row'=32,'col'=16] {'row'}, dimensions={1}, use_global_device_ids=true | all-gather | bytes 135168 | tf_op jit(solution)/shard_map/all_gather | solution.py:24
  161.1 0.6 gather_fusion
  161.7 0.0 copy-done
  161.7 0.9 fusion.6
  162.7 0.0 copy-start.7
  162.7 0.0 copy-done.6
  162.7 0.2 convolution_bitcast_fusion.3
  162.8 0.7 copy.42
  163.6 0.0 all-reduce.7.cloned.1.call-update
  163.6 0.0 all-reduce.9.cloned.1.call-start
  163.6 43.6 %all_gather.13 = bf16[8,4096]{1,0:T(8,128)(2,1)S(1)} all-gather(bf16[8,256]{1,0:T(8,128)(2,1)S(1)} %convert_element_type.19), channel_id=1, replica_groups=mesh['row'=32,'col'=16] {'col'}, dimensions={1}, use_global_device_ids=true | all-gather | bytes 69632 | tf_op jit(solution)/shard_map/all_gather | solution.py:25
  207.3 0.0 copy-start.1
  207.3 0.6 gather_fusion.1
  207.9 0.6 fusion.4
  208.4 0.0 copy-done.7
  208.5 0.3 convolution_bitcast_fusion.1
  208.7 0.8 copy.40
  209.6 0.0 all-reduce.9.cloned.1.call-update
  209.6 0.0 all-reduce.11.cloned.1.call-start
  209.7 152.3 %all-reduce.7.cloned.1.call-done = f32[8,4096]{1,0:T(8,128)} async-done(((f32[8,4096]{1,0:T(8,128)}), f32[8,4096]{1,0:T(8,128)}) %all-reduce.7.cloned.1.call-update) | async-done | bytes 131088 | tf_op jit(solution)/shard_map/psum | solution.py:49
  362.0 557.9 %all-reduce.9.cloned.1.call-done = f32[8,8192]{1,0:T(8,128)} async-done(((f32[8,8192]{1,0:T(8,128)}), f32[8,8192]{1,0:T(8,128)}) %all-reduce.9.cloned.1.call-update) | async-done | bytes 262160 | tf_op jit(solution)/shard_map/psum | solution.py:50
  919.8 0.0 copy-done.1
  919.8 0.9 multiply_reduce_fusion
  920.7 121.6 %all-reduce.1 = (f32[8]{0:T(128)S(1)}, f32[8]{0:T(128)S(1)}) all-reduce(f32[8]{0:T(128)S(1)} %get-tuple-element.7, f32[8]{0:T(128)S(1)} %get-tuple-element.6), channel_id=1, replica_groups=mesh['row'=32,'col'=16] {'row','col'}, use_global_device_ids=true, to_apply=%region_3.6 | all-reduce | flops 16 | bytes 128 | tf_op jit(solution)/shard_map/psum | solution.py:60
  1042.3 0.1 fusion.69
  1042.4 0.0 copy-start.2
  1042.4 31.7 %all_gather.15 = bf16[8,4096]{1,0:T(8,128)(2,1)S(1)} all-gather(bf16[8,256]{1,0:T(8,128)(2,1)S(1)} %get-tuple-element.12), channel_id=1, replica_groups=mesh['row'=32,'col'=16] {'col'}, dimensions={1}, use_global_device_ids=true | all-gather | bytes 69632 | tf_op jit(solution)/shard_map/all_gather | solution.py:25
  1074.0 136.6 %all_gather.14 = bf16[8,8192]{1,0:T(8,128)(2,1)S(1)} all-gather(bf16[8,256]{1,0:T(8,128)(2,1)S(1)} %get-tuple-element.12), channel_id=1, replica_groups=mesh['row'=32,'col'=16] {'row'}, dimensions={1}, use_global_device_ids=true | all-gather | bytes 135168 | tf_op jit(solution)/shard_map/all_gather | solution.py:24
  1210.6 0.6 gather_fusion.3
  1211.2 0.6 gather_fusion.2
  1211.8 0.9 fusion.2
  1212.8 0.2 convolution_bitcast_fusion.2
  1212.9 0.7 copy.41
  1213.6 0.0 copy-start.4
  1213.7 0.0 copy-start.5
  1213.7 0.0 all-reduce.11.cloned.1.call-update
  1213.7 0.0 all-reduce.13.cloned.1.call-start
  1213.7 0.6 fusion
  1214.3 0.3 convolution_bitcast_fusion
  1214.6 0.8 copy.39
  1215.4 0.0 all-reduce.13.cloned.1.call-update
  1215.5 0.0 copy-done.4
  1215.5 0.1 fusion.42
  1215.6 198.1 %all-reduce.11.cloned.1.call-done = f32[8,4096]{1,0:T(8,128)} async-done(((f32[8,4096]{1,0:T(8,128)}), f32[8,4096]{1,0:T(8,128)}) %all-reduce.11.cloned.1.call-update) | async-done | bytes 131088 | tf_op jit(solution)/shard_map/psum | solution.py:49
  1413.8 557.9 %all-reduce.13.cloned.1.call-done = f32[8,8192]{1,0:T(8,128)} async-done(((f32[8,8192]{1,0:T(8,128)}), f32[8,8192]{1,0:T(8,128)}) %all-reduce.13.cloned.1.call-update) | async-done | bytes 262160 | tf_op jit(solution)/shard_map/psum | solution.py:50
  1971.7 0.7 dynamic-slice_add_fusion
  1972.4 0.0 copy-done.2
  1972.4 0.0 copy-done.5
  1972.4 0.0 copy-start.3
  1972.4 0.1 fusion.32
  1972.6 121.9 %all-reduce = (f32[24,24]{1,0:T(8,128)S(1)}, f32[24,24]{1,0:T(8,128)S(1)}) all-reduce(f32[24,24]{1,0:T(8,128)S(1)} %fusion.42, f32[24,24]{1,0:T(8,128)S(1)} %fusion.32), channel_id=1, replica_groups=mesh['row'=32,'col'=16] {'row','col'}, use_global_device_ids=true, to_apply=%region_8.11 | all-reduce | flops 1152 | bytes 9216 | tf_op jit(solution)/shard_map/psum | solution.py:69
  2094.5 0.6 broadcast_multiply_fusion
  2095.1 0.0 copy-done.3
  (6 shorter events, 0.0 us)
Async XLA Ops:
  7.2 154.6 %copy-start = (bf16[1,1,48,128,128]{4,3,2,1,0:T(8,128)(2,1)S(1)}, bf16[1,1,48,128,128]{4,3,2,1,0:T(8,128)(2,1)}, u32[]{:S(2)}) copy-start(bf16[1,1,48,128,128]{4,3,2,1,0:T(8,128)(2,1)} %param.17) | copy-start | bytes 4718596
  7.2 155.5 %copy-start.6 = (s32[1,1,48]{2,1,0:T(1,128)S(1)}, s32[1,1,48]{2,1,0:T(1,128)}, u32[]{:S(2)}) copy-start(s32[1,1,48]{2,1,0:T(1,128)} %param.14) | copy-start | bytes 580
  7.2 354.8 %all-reduce.7.cloned.1.call-start = ((), (), s32[]{:S(2)}) async-start(), calls=%async_computation | async-start | bytes 262144 | tf_op jit(solution)/shard_map/psum | solution.py:49
  162.7 45.8 %copy-start.7 = (s32[1,1,48]{2,1,0:T(1,128)S(1)}, s32[1,1,48]{2,1,0:T(1,128)}, u32[]{:S(2)}) copy-start(s32[1,1,48]{2,1,0:T(1,128)} %param.15) | copy-start | bytes 580
  163.6 756.2 %all-reduce.9.cloned.1.call-start = ((), (), s32[]{:S(2)}) async-start(), calls=%async_computation.1 | async-start | bytes 524288 | tf_op jit(solution)/shard_map/psum | solution.py:50
  207.3 712.6 %copy-start.1 = (f32[8,256]{1,0:T(8,128)S(1)}, f32[8,256]{1,0:T(8,128)}, u32[]{:S(2)}) copy-start(f32[8,256]{1,0:T(8,128)} %param.11) | copy-start | bytes 24580
  209.6 1204.2 %all-reduce.11.cloned.1.call-start = ((), (), s32[]{:S(2)}) async-start(), calls=%async_computation.2 | async-start | bytes 262144 | tf_op jit(solution)/shard_map/psum | solution.py:49
  1042.4 930.0 %copy-start.2 = (f32[8,256]{1,0:T(8,128)}, f32[8,256]{1,0:T(8,128)S(1)}, u32[]{:S(2)}) copy-start(f32[8,256]{1,0:T(8,128)S(1)} %get-tuple-element.13) | copy-start | bytes 24580
  1213.6 1.8 copy-start.4
  1213.7 758.8 %copy-start.5 = (f32[8,256]{1,0:T(8,128)S(1)}, f32[8,256]{1,0:T(8,128)}, u32[]{:S(2)}) copy-start(f32[8,256]{1,0:T(8,128)} %param.13) | copy-start | bytes 24580
  1213.7 758.0 %all-reduce.13.cloned.1.call-start = ((), (), s32[]{:S(2)}) async-start(), calls=%async_computation.3 | async-start | bytes 524288 | tf_op jit(solution)/shard_map/psum | solution.py:50
  1972.4 122.7 %copy-start.3 = (f32[8,256]{1,0:T(8,128)}, f32[8,256]{1,0:T(8,128)S(1)}, u32[]{:S(2)}) copy-start(f32[8,256]{1,0:T(8,128)S(1)} %dynamic-slice_add_fusion) | copy-start | bytes 24580
Sparse Core Ops, SparseCore 0:
  163.7 198.1 all-reduce.6
  365.1 554.6 all-reduce.8
  1213.8 199.9 all-reduce.10
  1416.8 554.8 all-reduce.12
where the time goes:
time: 2100 us
  waiting for transfers between devices  1470 us (70%)
  blocking collectives  606 us (29%)
    psum x2, waiting for transfers between devices, apply_hamiltonian(): col_total = lax.psum(col_part, 'row')  1120 us
    psum x2, waiting for transfers between devices, apply_hamiltonian(): row_total = lax.psum(row_part, 'col')  350 us
    all_gather x2, blocking collectives, apply_hamiltonian(): column_group = lax.all_gather(rounded, 'row', axis=1, tiled=True)  288 us
    psum x1, blocking collectives, body(): lax.psum((inner_products(stacked, stacked), inner_products(stacked, image...  122 us
    psum x1, blocking collectives, body(): lax.psum((jnp.sum(x_block * hx_block, axis=1), jnp.sum(x_block * x_block,...  122 us
    all_gather x2, blocking collectives, apply_hamiltonian(): row_group = lax.all_gather(rounded, 'col', axis=1, tiled=True)  75.3 us
  transfers between devices with their start and end apart: 4, of which 4 were waited for; matrix products, arithmetic and copies ran while one was open for 0% of the time, Pallas kernels for 0%

commit v1 on v0

v1 whole, which is shorter than its diff:
```python
import jax
import jax.numpy as jnp
from jax import lax
from jax.experimental import pallas as pl
from jax.experimental.pallas import tpu as pltpu
from jax.sharding import PartitionSpec as P

MESH = pl.DeviceIdType.MESH
F32 = jnp.float32
BF16 = jnp.bfloat16
SLOTS = 48
UNROLL = 16
NT = (((1,), (1,)), ((), ()))
PLANE = sorted(
    [(dy, dx) for dy in range(4) for dx in range(4) if (dy, dx) != (0, 0)],
    key=lambda o: -(min(o[0], 4 - o[0]) + min(o[1], 4 - o[1])),
)
RING = [8] + [d for k in range(7, 0, -1) for d in (k, 16 - k)]


def kernel(
    x_hbm, p_hbm, hp_hbm, rows_hbm, cols_hbm, count_hbm, tiles_hbm,
    res_out, img_out, gs_out, gh_out,
    xv, pv, hpv, rows_v, cols_v, rows_s, cols_s, count_s, tiles,
    hot_f, hot_b, prod, rowx, colx, row_send, row_recv, col_send, col_recv,
    part_send, part_recv, stack, images, partner_x,
    th1, th2, early_send, early1, early2, early3, late1, late2,
    local_sem, send_sem, recv_sem,
):
    r = lax.axis_index("row")
    c = lax.axis_index("col")
    zh = lax.rem(r, 2)
    q = lax.div(r, 2)
    y, xx = lax.div(q, 4), lax.rem(q, 4)
    core = lax.rem(c, 2)
    z = zh * 8 + lax.div(c, 2)
    mate = r + 1 - 2 * zh
    partner = (mate, c)
    zslot = zh * 16 + c

    plane_peers = []
    for dy, dx in PLANE:
        other = lax.rem(y + dy, 4) * 4 + lax.rem(xx + dx, 4)
        plane_peers.append((other, (other * 2 + zh, c)))
    line_peers = []
    for k in range(15):
        down = 15 - k
        down = down - jnp.where(down <= c, 1, 0)
        up = k + jnp.where(k >= c, 1, 0)
        other = jnp.where(c < 8, down, up)
        line_peers.append((other, (r, other)))
    ring_peers = []
    for d in RING:
        oz = lax.rem(z + d, 16)
        orow = q * 2 + lax.div(oz, 8)
        for k in range(2):
            ring_peers.append((orow, lax.rem(oz, 8) * 2 + k))
    ring_peers.append((r, c + 1 - 2 * core))

    barrier = pltpu.get_barrier_semaphore()
    for device in ring_peers:
        pl.semaphore_signal(barrier, inc=1, device_id=device, device_id_type=MESH)
    for _, device in plane_peers:
        pl.semaphore_signal(barrier, inc=1, device_id=device, device_id_type=MESH)

    loads = [
        pltpu.make_async_copy(src, dst, local_sem.at[i])
        for i, (src, dst) in enumerate(
            [
                (x_hbm, xv), (rows_hbm, rows_v), (cols_hbm, cols_v), (count_hbm, count_s),
                (rows_hbm, rows_s), (cols_hbm, cols_s), (tiles_hbm, tiles), (p_hbm, pv), (hp_hbm, hpv),
            ]
        )
    ]
    for load in loads:
        load.start()

    def send(src, dst, which, device):
        pltpu.make_async_remote_copy(
            src_ref=src, dst_ref=dst, send_sem=send_sem.at[which], recv_sem=recv_sem.at[which],
            device_id=device, device_id_type=MESH,
        ).start()

    def wait_on(sem, ref):
        pltpu.make_async_copy(ref, ref, sem).wait()

    sent = []

    def arrived(which, ref):
        wait_on(recv_sem.at[which], ref)
        sent.append((which, ref))

    def fold(wide):
        return jnp.concatenate([wide[:, :128], wide[:, 128:]], axis=0)

    def unfold(tall):
        return jnp.concatenate([tall[:8], tall[8:]], axis=1)

    loads[0].wait()
    x_tall = fold(xv[...])
    x_round = x_tall.astype(BF16)
    rowx[0, c] = x_round
    colx[0, r] = x_round

    for i in (1, 2, 3):
        loads[i].wait()
    sub = lax.broadcasted_iota(jnp.int32, (16, SLOTS), 0)
    lane = lax.broadcasted_iota(jnp.int32, (16, SLOTS), 1)
    alive = jnp.where(lane < count_s[0, 0], 1.0, 0.0)
    table = jnp.where(
        sub == 0, rows_v[0].astype(F32), jnp.where(sub == 1, cols_v[0].astype(F32), alive)
    ).astype(BF16)
    spread = jnp.where(
        lax.div(lax.broadcasted_iota(jnp.int32, (SLOTS, SLOTS * 16), 1), 16)
        == lax.broadcasted_iota(jnp.int32, (SLOTS, SLOTS * 16), 0),
        1.0, 0.0,
    ).astype(BF16)
    wide = jnp.dot(table, spread, preferred_element_type=F32).astype(jnp.int32)
    row_id, col_id, on = wide[0:1], wide[1:2], wide[2:3]
    pos = lax.broadcasted_iota(jnp.int32, (1, SLOTS * 16), 1)
    vec = lax.rem(pos, 8)
    half = lax.rem(lax.div(pos, 8), 2)
    key_f = jnp.where((on == 1) & (lax.rem(col_id, 2) == half), row_id * 8 + vec, -1)
    key_b = jnp.where((on == 1) & (lax.rem(row_id, 2) == half), col_id * 8 + vec, -1)
    strip = lax.broadcasted_iota(jnp.int32, (16, SLOTS * 16), 0)

    def fill_f(i, carry):
        hot_f[pl.ds(pl.multiple_of(i * 16, 16), 16), :] = jnp.where(strip + i * 16 == key_f, 1.0, 0.0).astype(BF16)
        return carry

    def fill_b(i, carry):
        hot_b[pl.ds(pl.multiple_of(i * 16, 16), 16), :] = jnp.where(strip + i * 16 == key_b, 1.0, 0.0).astype(BF16)
        return carry

    lax.fori_loop(0, 16, fill_f, 0)
    lax.fori_loop(0, 32, fill_b, 0)
    for i in range(4, 9):
        loads[i].wait()

    pl.semaphore_wait(barrier, len(ring_peers) + len(plane_peers))

    def send_gather(k):
        base = 8 * k
        send(colx.at[k, r], colx.at[k, r], base + 1, partner)
        for _, device in line_peers:
            send(rowx.at[k, c], rowx.at[k, c], base, device)
        for _, device in plane_peers:
            send(colx.at[k, r], colx.at[k, r], base + 2, device)

    def forward_partner(k):
        base = 8 * k
        arrived(base + 1, colx.at[k, mate])
        for _, device in plane_peers:
            send(colx.at[k, mate], colx.at[k, mate], base + 3, device)

    def products(k, index, source, dims):
        def step(i, carry):
            for u in range(UNROLL):
                t = i * UNROLL + u
                block = source[k, lax.div(index[0, 0, t], 2)]
                out = lax.dot_general(block, tiles[0, 0, t], dims, preferred_element_type=F32)
                prod[pl.ds(pl.multiple_of(t * 16, 16), 16), :] = out.astype(BF16)
            return carry

        lax.fori_loop(0, SLOTS // UNROLL, step, 0)

    def transposed_part(k):
        base = 8 * k
        arrived(base, rowx.at[k, pl.ds(0, 15)])
        products(k, rows_s, rowx, (((1,), (0,)), ((), ())))
        for g in range(4):
            part = jnp.dot(hot_b[pl.ds(g * 128, 128), :], prod[...], preferred_element_type=F32)
            col_send[k, pl.ds(g * 4, 4)] = part.astype(BF16).reshape(4, 32, 128)
        col_recv[k, q] = col_send[k, q]
        for other, device in plane_peers:
            send(col_send.at[k, other], col_recv.at[k, q], base + 4, device)

    def forward_part(k):
        base = 8 * k
        arrived(base + 2, colx.at[k, pl.ds(0, 15)])
        arrived(base + 3, colx.at[k, pl.ds(0, 15)])
        products(k, cols_s, colx, NT)
        for g in range(2):
            part = jnp.dot(hot_f[pl.ds(g * 128, 128), :], prod[...], preferred_element_type=F32)
            row_send[k, pl.ds(g * 8, 8)] = part.astype(BF16).reshape(8, 16, 128)
        row_recv[k, c] = row_send[k, c]
        for other, device in line_peers:
            send(row_send.at[k, other], row_recv.at[k, c], base + 5, device)

    def total(ref, k, n):
        out = ref[k, 0].astype(F32)
        for i in range(1, n):
            out = out + ref[k, i].astype(F32)
        return out

    def column_sums(k):
        base = 8 * k
        arrived(base + 4, col_recv.at[k, pl.ds(0, 15)])
        both = total(col_recv, k, 16)
        mine = jnp.where(zh == 0, both[:16], both[16:])
        theirs = jnp.where(zh == 0, both[16:], both[:16])
        part_send[k] = theirs
        send(part_send.at[k], part_recv.at[k], base + 6, partner)
        return mine, theirs

    def finish(k, mine):
        base = 8 * k
        arrived(base + 5, row_recv.at[k, pl.ds(0, 15)])
        out = mine + total(row_recv, k, 16)
        arrived(base + 6, part_recv.at[k])
        return out + part_recv[k]

    send_gather(0)
    send(xv, partner_x, 16, partner)
    stack[0:8] = xv[...]
    stack[16:24] = pv[...]
    images[24:32] = hpv[...]
    forward_partner(0)
    transposed_part(0)
    forward_part(0)
    mine, theirs = column_sums(0)

    arrived(16, partner_x)
    weighted = x_tall * mine + fold(partner_x[...]) * theirs
    squared = x_tall * x_tall
    num = jnp.sum(weighted[:8] + weighted[8:], axis=1, keepdims=True)
    den = jnp.sum(squared[:8] + squared[8:], axis=1, keepdims=True)
    sub8 = lax.broadcasted_iota(jnp.int32, (8, 128), 0)
    lane8 = lax.broadcasted_iota(jnp.int32, (8, 128), 1)
    placed = jnp.where(lane8 == sub8, num, jnp.where(lane8 == sub8 + 8, den, 0.0))
    th1[q] = jnp.sum(placed, axis=0, keepdims=True)
    for _, device in plane_peers:
        send(th1.at[q], th1.at[q], 17, device)
    arrived(17, th1.at[pl.ds(0, 15)])
    acc = th1[0]
    for i in range(1, 16):
        acc = acc + th1[i]
    th2[zslot] = acc
    for device in ring_peers:
        send(th2.at[zslot], th2.at[zslot], 18, device)
    hx_tall = finish(0, mine)
    arrived(18, th2.at[pl.ds(0, 31)])
    acc = th2[0]
    for i in range(1, 32):
        acc = acc + th2[i]
    num = 2.0 * jnp.sum(jnp.where(lane8 == sub8, acc, 0.0), axis=1, keepdims=True)
    den = jnp.sum(jnp.where(lane8 == sub8 + 8, acc, 0.0), axis=1, keepdims=True)
    theta = num / den
    theta_tall = jnp.concatenate([theta, theta], axis=0)
    res_tall = hx_tall - theta_tall * x_tall
    res_round = res_tall.astype(BF16)
    rowx[1, c] = res_round
    colx[1, r] = res_round

    send_gather(1)
    residual = unfold(res_tall)
    res_out[...] = residual
    stack[8:16] = residual
    images[0:24] = stack[...]
    images[32:40] = unfold(hx_tall)
    early = lax.dot_general(
        stack[...], images[...], NT, precision=lax.Precision.HIGHEST, preferred_element_type=F32
    )
    early = jnp.concatenate([early, jnp.zeros((24, 88), F32)], axis=1)
    for i in range(12):
        early_send[i] = early[2 * i : 2 * i + 2]
    for i in range(12, 16):
        early_send[i] = jnp.zeros((2, 128), F32)
    early1[q] = early_send[q]
    for other, device in plane_peers:
        send(early_send.at[other], early1.at[q], 19, device)
    forward_partner(1)
    transposed_part(1)
    arrived(19, early1.at[pl.ds(0, 15)])
    acc = early1[0]
    for i in range(1, 16):
        acc = acc + early1[i]
    early2[zslot] = acc
    for device in ring_peers:
        send(early2.at[zslot], early2.at[zslot], 20, device)
    forward_part(1)
    mine, theirs = column_sums(1)
    arrived(20, early2.at[pl.ds(0, 31)])
    acc = early2[0]
    for i in range(1, 32):
        acc = acc + early2[i]
    early3[q] = acc
    for _, device in plane_peers:
        send(early3.at[q], early3.at[q], 21, device)
    img_tall = finish(1, mine)
    image = unfold(img_tall)
    img_out[...] = image

    late = lax.dot_general(
        stack[...], image, NT, precision=lax.Precision.HIGHEST, preferred_element_type=F32
    )
    late = jnp.concatenate([late, jnp.zeros((24, 120), F32)], axis=1)
    packed = late[0:8] + pltpu.roll(late[8:16], 8, 1) + pltpu.roll(late[16:24], 16, 1)
    lines = jnp.where(lax.rem(sub8, 4) == 0, packed, 0.0)
    for k in range(1, 4):
        lines = lines + jnp.where(lax.rem(sub8, 4) == k, pltpu.roll(packed, 32 * k, 1), 0.0)
    late1[q] = jnp.concatenate(
        [jnp.sum(lines[0:4], axis=0, keepdims=True), jnp.sum(lines[4:8], axis=0, keepdims=True)], axis=0
    )
    for _, device in plane_peers:
        send(late1.at[q], late1.at[q], 22, device)
    arrived(22, late1.at[pl.ds(0, 15)])
    acc = late1[0]
    for i in range(1, 16):
        acc = acc + late1[i]
    late2[zslot] = acc
    for device in ring_peers:
        send(late2.at[zslot], late2.at[zslot], 23, device)

    cells = 1.0 / 131072.0
    arrived(21, early3.at[pl.ds(0, 15)])
    rows = [early3[i] for i in range(12)]
    early = jnp.concatenate(rows, axis=0) * cells
    gs_out[...] = early[:, :24]
    shifted = pltpu.roll(early, 128 - 32, 1)
    hp_part = pltpu.roll(early, 128 - 8, 1)

    arrived(23, late2.at[pl.ds(0, 31)])
    acc = late2[0]
    for i in range(1, 32):
        acc = acc + late2[i]
    acc = acc * cells
    spread8 = jnp.where(sub8 < 4, acc[0:1], acc[1:2])
    packed = jnp.where(lax.rem(sub8, 4) == 0, spread8, 0.0)
    for k in range(1, 4):
        packed = packed + jnp.where(lax.rem(sub8, 4) == k, pltpu.roll(spread8, 128 - 32 * k, 1), 0.0)
    for a in range(3):
        block = pltpu.roll(packed, 136 - 8 * a if a > 1 else 8 - 8 * a, 1) if a != 1 else packed
        low = shifted[8 * a : 8 * a + 8]
        high = hp_part[8 * a : 8 * a + 8]
        block = jnp.where(lane8 < 8, low, jnp.where(lane8 < 16, block, high))
        gh_out[8 * a : 8 * a + 8, :] = block[:, :24]

    for which, ref in sent:
        wait_on(send_sem.at[which], ref)


def solution(mesh):
    def body(x_block, p_block, hp_block, tile_rows, tile_cols, tile_count, tile_values):
        any_spec = pl.BlockSpec(memory_space=pl.ANY)
        vmem = pl.BlockSpec(memory_space=pltpu.VMEM)
        return pl.pallas_call(
            kernel,
            out_shape=(
                jax.ShapeDtypeStruct((8, 256), F32),
                jax.ShapeDtypeStruct((8, 256), F32),
                jax.ShapeDtypeStruct((24, 24), F32),
                jax.ShapeDtypeStruct((24, 24), F32),
            ),
            in_specs=[any_spec] * 7,
            out_specs=(vmem,) * 4,
            scratch_shapes=[
                pltpu.VMEM((8, 256), F32), pltpu.VMEM((8, 256), F32), pltpu.VMEM((8, 256), F32),
                pltpu.VMEM((1, 1, SLOTS), jnp.int32), pltpu.VMEM((1, 1, SLOTS), jnp.int32),
                pltpu.SMEM((1, 1, SLOTS), jnp.int32), pltpu.SMEM((1, 1, SLOTS), jnp.int32),
                pltpu.SMEM((1, 1), jnp.int32),
                pltpu.VMEM((1, 1, SLOTS, 128, 128), BF16),
                pltpu.VMEM((256, SLOTS * 16), BF16), pltpu.VMEM((512, SLOTS * 16), BF16),
                pltpu.VMEM((SLOTS * 16, 128), BF16),
                pltpu.VMEM((2, 16, 16, 128), BF16), pltpu.VMEM((2, 32, 16, 128), BF16),
                pltpu.VMEM((2, 16, 16, 128), BF16), pltpu.VMEM((2, 16, 16, 128), BF16),
                pltpu.VMEM((2, 16, 32, 128), BF16), pltpu.VMEM((2, 16, 32, 128), BF16),
                pltpu.VMEM((2, 16, 128), F32), pltpu.VMEM((2, 16, 128), F32),
                pltpu.VMEM((24, 256), F32), pltpu.VMEM((40, 256), F32), pltpu.VMEM((8, 256), F32),
                pltpu.VMEM((16, 1, 128), F32), pltpu.VMEM((32, 1, 128), F32),
                pltpu.VMEM((16, 2, 128), F32), pltpu.VMEM((16, 2, 128), F32),
                pltpu.VMEM((32, 2, 128), F32), pltpu.VMEM((16, 2, 128), F32),
                pltpu.VMEM((16, 2, 128), F32), pltpu.VMEM((32, 2, 128), F32),
                pltpu.SemaphoreType.DMA((9,)), pltpu.SemaphoreType.DMA((24,)), pltpu.SemaphoreType.DMA((24,)),
            ],
            compiler_params=pltpu.CompilerParams(
                collective_id=0, has_side_effects=True, vmem_limit_bytes=32 * 1024 * 1024
            ),
        )(x_block, p_block, hp_block, tile_rows, tile_cols, tile_count, tile_values)

    in_specs = (
        P(None, ("row", "col")),
        P(None, ("row", "col")),
        P(None, ("row", "col")),
        P("row", "col", None),
        P("row", "col", None),
        P("row", "col"),
        P("row", "col", None, None, None),
    )
    out_specs = (P(None, ("row", "col")), P(None, ("row", "col")), P(), P())
    return jax.shard_map(body, mesh=mesh, in_specs=in_specs, out_specs=out_specs, check_vma=False)
```

time: 2100 us -> 84.7 us (0.04)
  waiting for transfers between devices: 1470 us -> 0 us
  blocking collectives: 606 us -> 0 us
  Pallas kernels: 0 us -> 75.9 us
    psum x4 -> x0, waiting for transfers between devices: 1470 us -> none  [the longest x2 1120 us: apply_hamiltonian(): col_total = lax.psum(col_part, 'row')]
    all_gather x4 -> x0, blocking collectives: 363 us -> none  [the longest x2 288 us: apply_hamiltonian(): column_group = lax.all_gather(rounded, 'row', axis=1, tiled=True)]
    psum x2 -> x0, blocking collectives: 244 us -> none  [the longest x1 122 us: body(): lax.psum((inner_products(stacked, stacked), inner_products(stacked, image...]
    pallas_call x0 -> x1, Pallas kernels: none -> 75.9 us  [body(): pl.pallas_call(kernel, out_shape=(jax.ShapeDtypeStruct((8, 256), F32), ja...]
  transfers between devices with their start and end apart: 4 -> 0, of which waited for: 4 -> 0; matrix products, arithmetic and copies ran while one was open for 0% -> 0% of each run, Pallas kernels for 0% -> 0%
where the time goes in v1:
time: 84.7 us; the launch traced here: 84.4 us
  Pallas kernels  75.9 us (90%)
  local copies, waits for them, and re-layouts  7.2 us (9%)
  between operations  1.3 us (2%)
    pallas_call x1, Pallas kernels, body(): pl.pallas_call(kernel, out_shape=(jax.ShapeDtypeStruct((8, 256), F32), ja...  75.9 us
    unnamed x16, local copies, waits for them, and re-layouts  7.2 us

profile of v1, /device:TPU:1, one launch (start us, length us, event | category | flops | bytes accessed | tf_op | source)
XLA Modules:
  0.0 84.4 jit_solution(9591319599972476872)
XLA Ops:
  1.3 0.0 copy-start
  1.3 1.4 %copy-done = bf16[1,1,48,128,128]{4,3,2,1,0:T(8,128)(2,1)S(1)} copy-done((bf16[1,1,48,128,128]{4,3,2,1,0:T(8,128)(2,1)S(1)}, bf16[1,1,48,128,128]{4,3,2,1,0:T(8,128)(2,1)}, u32[]{:S(2)}) %copy-start) | copy-done | bytes 1572888
  2.7 0.0 copy-start.1
  2.7 0.7 copy-done.1
  3.4 0.0 copy-start.2
  3.4 0.7 copy-done.2
  4.1 0.0 copy-start.3
  4.1 0.7 copy-done.3
  4.8 0.0 copy-start.4
  4.8 0.7 copy-done.4
  5.4 0.0 copy-start.5
  5.4 0.7 copy-done.5
  6.1 75.9 %shard_map.102 = (f32[8,256]{1,0:T(8,128)S(1)}, f32[8,256]{1,0:T(8,128)S(1)}, f32[24,24]{1,0:T(8,128)S(1)}, f32[24,24]{1,0:T(8,128)S(1)}) custom-call(f32[8,256]{1,0:T(8,128)S(1)} %copy-done.1, f32[8,256]{1,0:T(8,128)S(1)} %copy-done.2, f32[8,256]{1,0:T(8,128)S(1)} %copy-done.3, s32[1,1,48]{2,1,0:T(1,128)S(1)} %copy-done.4, s32[1,1,48]{2,1,0:T(1,128)S(1)} %copy-done.5, ...), custom_call_target="tpu_custom_call" | custom-call | tf_op jit(solution)/shard_map/pallas_call | solution.py:347
  82.0 0.6 copy.16
  82.6 0.6 copy.17
  83.2 0.6 copy.18
  83.8 0.6 copy.19
Async XLA Ops:
  1.3 1.4 %copy-start = (bf16[1,1,48,128,128]{4,3,2,1,0:T(8,128)(2,1)S(1)}, bf16[1,1,48,128,128]{4,3,2,1,0:T(8,128)(2,1)}, u32[]{:S(2)}) copy-start(bf16[1,1,48,128,128]{4,3,2,1,0:T(8,128)(2,1)} %tiles_hbm.1) | copy-start | bytes 4718596
  2.7 0.7 copy-start.1
  3.4 0.7 copy-start.2
  4.1 0.7 copy-start.3
  4.8 0.7 copy-start.4
  5.4 0.7 copy-start.5

commit v2 on v1

v2 whole, which is shorter than its diff:
```python
import jax
import jax.numpy as jnp
from jax import lax
from jax.experimental import pallas as pl
from jax.experimental.pallas import tpu as pltpu
from jax.sharding import PartitionSpec as P

MESH = pl.DeviceIdType.MESH
F32 = jnp.float32
BF16 = jnp.bfloat16
SLOTS = 48
UNROLL = 16
VMEM_LIMIT = 60 * 1024 * 1024
NN = (((1,), (0,)), ((), ()))
NT = (((1,), (1,)), ((), ()))
def kernel(
    x_hbm, p_hbm, hp_hbm, rows_hbm, cols_hbm, count_hbm, tiles_hbm,
    res_out, img_out, gs_out, gh_out,
    xv, pv, hpv, rows_v, cols_v, rows_s, cols_s, count_s, tiles,
    hot_f, hot_b, prod, rowx, colx, row_send, row_recv, col_send, col_recv,
    part_send, part_recv, stack, images, partner_x, partner_p, rowp, colp_send, colp_recv,
    th1, th2, early_send, early1, early2, early3, late1, late2,
    local_sem, send_sem, recv_sem,
):
    r = lax.axis_index("row")
    c = lax.axis_index("col")
    zh = lax.rem(r, 2)
    q = lax.div(r, 2)
    y, xx = lax.div(q, 4), lax.rem(q, 4)
    core = lax.rem(c, 2)
    z = zh * 8 + lax.div(c, 2)
    mate = r + 1 - 2 * zh
    partner = (mate, c)
    zslot = zh * 16 + c

    def each_plane(act):
        def step(i, carry):
            a, b = lax.div(i, 4), lax.rem(i, 4)
            dy = jnp.where(a < 2, 2 - a, 9 - 3 * a)
            dx = jnp.where(b < 2, 2 - b, 9 - 3 * b)
            other = lax.rem(y + dy, 4) * 4 + lax.rem(xx + dx, 4)
            act(other, (other * 2 + zh, c))
            return carry

        lax.fori_loop(0, 15, step, 0)

    def each_line(act):
        def step(i, carry):
            down = 15 - i - jnp.where(15 - i <= c, 1, 0)
            up = i + jnp.where(i >= c, 1, 0)
            other = jnp.where(c < 8, down, up)
            act(other, (r, other))
            return carry

        lax.fori_loop(0, 15, step, 0)

    def each_ring(act):
        def step(i, carry):
            m = lax.div(i, 2)
            s = lax.div(m + 1, 2)
            d = 8 + jnp.where(lax.rem(m, 2) == 0, s, -s)
            oz = lax.rem(z + d, 16)
            k = jnp.where(m == 15, 1 - core, lax.rem(i, 2))
            act((q * 2 + lax.div(oz, 8), lax.rem(oz, 8) * 2 + k))
            return carry

        lax.fori_loop(0, 31, step, 0)

    barrier = pltpu.get_barrier_semaphore()

    def greet(device):
        pl.semaphore_signal(barrier, inc=1, device_id=device, device_id_type=MESH)

    each_ring(greet)
    each_plane(lambda other, device: greet(device))

    loads = [
        pltpu.make_async_copy(src, dst, local_sem.at[i])
        for i, (src, dst) in enumerate(
            [
                (x_hbm, xv), (rows_hbm, rows_v), (cols_hbm, cols_v), (count_hbm, count_s),
                (rows_hbm, rows_s), (cols_hbm, cols_s), (tiles_hbm, tiles), (p_hbm, pv), (hp_hbm, hpv),
            ]
        )
    ]
    for load in loads:
        load.start()

    def send(src, dst, which, device):
        pltpu.make_async_remote_copy(
            src_ref=src, dst_ref=dst, send_sem=send_sem.at[which], recv_sem=recv_sem.at[which],
            device_id=device, device_id_type=MESH,
        ).start()

    def wait_on(sem, ref):
        pltpu.make_async_copy(ref, ref, sem).wait()

    sent = []

    def arrived(which, ref):
        wait_on(recv_sem.at[which], ref)
        sent.append((which, ref))

    def exact(a, b):
        return lax.dot_general(a, b, NT, precision=lax.Precision.HIGHEST, preferred_element_type=F32)

    def fold(wide):
        return jnp.concatenate([wide[:, :128], wide[:, 128:]], axis=0)

    def unfold(tall):
        return jnp.concatenate([tall[:8], tall[8:]], axis=1)

    loads[0].wait()
    x_tall = fold(xv[...])
    x_round = x_tall.astype(BF16)
    rowx[0, c] = x_round
    loads[7].wait()
    rowp[c] = fold(pv[...]).astype(BF16)
    colx[0, r] = x_round

    for i in (1, 2, 3):
        loads[i].wait()
    sub = lax.broadcasted_iota(jnp.int32, (16, SLOTS), 0)
    lane = lax.broadcasted_iota(jnp.int32, (16, SLOTS), 1)
    alive = jnp.where(lane < count_s[0, 0], 1.0, 0.0)
    table = jnp.where(
        sub == 0, rows_v[0].astype(F32), jnp.where(sub == 1, cols_v[0].astype(F32), alive)
    ).astype(BF16)
    spread = jnp.where(
        lax.div(lax.broadcasted_iota(jnp.int32, (SLOTS, SLOTS * 16), 1), 16)
        == lax.broadcasted_iota(jnp.int32, (SLOTS, SLOTS * 16), 0),
        1.0, 0.0,
    ).astype(BF16)
    wide = jnp.dot(table, spread, preferred_element_type=F32).astype(jnp.int32)
    row_id, col_id, on = wide[0:1], wide[1:2], wide[2:3]
    pos = lax.broadcasted_iota(jnp.int32, (1, SLOTS * 16), 1)
    vec = lax.rem(pos, 8)
    half = lax.rem(lax.div(pos, 8), 2)
    key_f = jnp.where((on == 1) & (lax.rem(col_id, 2) == half), row_id * 8 + vec, -1)
    key_b = jnp.where((on == 1) & (lax.rem(row_id, 2) == half), col_id * 8 + vec, -1)
    strip = lax.broadcasted_iota(jnp.int32, (16, SLOTS * 16), 0)

    def fill_f(i, carry):
        hot_f[pl.ds(pl.multiple_of(i * 16, 16), 16), :] = jnp.where(strip + i * 16 == key_f, 1.0, 0.0).astype(BF16)
        return carry

    def fill_b(i, carry):
        hot_b[pl.ds(pl.multiple_of(i * 16, 16), 16), :] = jnp.where(strip + i * 16 == key_b, 1.0, 0.0).astype(BF16)
        return carry

    lax.fori_loop(0, 16, fill_f, 0)
    lax.fori_loop(0, 32, fill_b, 0)
    for i in (4, 5, 6, 8):
        loads[i].wait()

    pl.semaphore_wait(barrier, 46)

    def send_gather(k):
        base = 8 * k
        send(colx.at[k, r], colx.at[k, r], base + 1, partner)
        each_line(lambda other, device: send(rowx.at[k, c], rowx.at[k, c], base, device))
        each_plane(lambda other, device: send(colx.at[k, r], colx.at[k, r], base + 2, device))

    def forward_partner(k):
        base = 8 * k
        arrived(base + 1, colx.at[k, mate])
        each_plane(lambda other, device: send(colx.at[k, mate], colx.at[k, mate], base + 3, device))

    def products(index, source, dims):
        def step(i, carry):
            for u in range(UNROLL):
                t = i * UNROLL + u
                block = source[lax.div(index[0, 0, t], 2)]
                out = lax.dot_general(block, tiles[0, 0, t], dims, preferred_element_type=F32)
                prod[pl.ds(pl.multiple_of(t * 16, 16), 16), :] = out.astype(BF16)
            return carry

        lax.fori_loop(0, SLOTS // UNROLL, step, 0)

    def to_columns(out):
        for g in range(4):
            part = jnp.dot(hot_b[pl.ds(g * 128, 128), :], prod[...], preferred_element_type=F32)
            out[pl.ds(g * 4, 4)] = part.astype(BF16).reshape(4, 32, 128)

    def transposed_part(k):
        base = 8 * k
        arrived(base, rowx.at[k, pl.ds(0, 15)])
        products(rows_s, rowx.at[k], NN)
        to_columns(col_send.at[k])
        col_recv[k, q] = col_send[k, q]
        each_plane(lambda other, device: send(col_send.at[k, other], col_recv.at[k, q], base + 4, device))

    def forward_part(k):
        base = 8 * k
        arrived(base + 2, colx.at[k, pl.ds(0, 15)])
        arrived(base + 3, colx.at[k, pl.ds(0, 15)])
        products(cols_s, colx.at[k], NT)
        for g in range(2):
            part = jnp.dot(hot_f[pl.ds(g * 128, 128), :], prod[...], preferred_element_type=F32)
            row_send[k, pl.ds(g * 8, 8)] = part.astype(BF16).reshape(8, 16, 128)
        row_recv[k, c] = row_send[k, c]
        each_line(lambda other, device: send(row_send.at[k, other], row_recv.at[k, c], base + 5, device))

    def total(ref, n):
        out = ref[0].astype(F32)
        for i in range(1, n):
            out = out + ref[i].astype(F32)
        return out

    def split(both):
        return jnp.where(zh == 0, both[:16], both[16:]), jnp.where(zh == 0, both[16:], both[:16])

    def column_sums(k):
        base = 8 * k
        arrived(base + 4, col_recv.at[k, pl.ds(0, 15)])
        mine, theirs = split(total(col_recv.at[k], 16))
        part_send[k] = theirs
        send(part_send.at[k], part_recv.at[k], base + 6, partner)
        return mine, theirs

    def finish(k, mine):
        base = 8 * k
        arrived(base + 5, row_recv.at[k, pl.ds(0, 15)])
        out = mine + total(row_recv.at[k], 16)
        arrived(base + 6, part_recv.at[k])
        return out + part_recv[k]

    send_gather(0)
    send(xv, partner_x, 16, partner)
    send(pv, partner_p, 24, partner)
    each_line(lambda other, device: send(rowp.at[c], rowp.at[c], 25, device))
    stack[0:8] = xv[...]
    stack[16:24] = pv[...]
    images[24:32] = hpv[...]
    forward_partner(0)
    transposed_part(0)
    forward_part(0)
    mine, theirs = column_sums(0)

    arrived(16, partner_x)
    weighted = x_tall * mine + fold(partner_x[...]) * theirs
    squared = x_tall * x_tall
    num = jnp.sum(weighted[:8] + weighted[8:], axis=1, keepdims=True)
    den = jnp.sum(squared[:8] + squared[8:], axis=1, keepdims=True)
    sub8 = lax.broadcasted_iota(jnp.int32, (8, 128), 0)
    lane8 = lax.broadcasted_iota(jnp.int32, (8, 128), 1)
    placed = jnp.where(lane8 == sub8, num, jnp.where(lane8 == sub8 + 8, den, 0.0))
    th1[q] = jnp.sum(placed, axis=0, keepdims=True)
    each_plane(lambda other, device: send(th1.at[q], th1.at[q], 17, device))
    arrived(17, th1.at[pl.ds(0, 15)])
    acc = total(th1, 16)
    th2[zslot] = acc
    each_ring(lambda device: send(th2.at[zslot], th2.at[zslot], 18, device))

    arrived(25, rowp.at[pl.ds(0, 15)])
    products(rows_s, rowp, NN)
    to_columns(colp_send)
    colp_recv[q] = colp_send[q]
    each_plane(lambda other, device: send(colp_send.at[other], colp_recv.at[q], 26, device))

    hx_tall = finish(0, mine)
    arrived(18, th2.at[pl.ds(0, 31)])
    acc = total(th2, 32)
    num = 2.0 * jnp.sum(jnp.where(lane8 == sub8, acc, 0.0), axis=1, keepdims=True)
    den = jnp.sum(jnp.where(lane8 == sub8 + 8, acc, 0.0), axis=1, keepdims=True)
    theta = num / den
    theta_tall = jnp.concatenate([theta, theta], axis=0)
    res_tall = hx_tall - theta_tall * x_tall
    res_round = res_tall.astype(BF16)
    rowx[1, c] = res_round
    colx[1, r] = res_round

    send_gather(1)
    residual = unfold(res_tall)
    res_out[...] = residual
    stack[8:16] = residual
    stack[24:32] = unfold(hx_tall)
    images[0:24] = stack[0:24]
    images[32:40] = stack[24:32]
    images[40:48] = unfold(res_round.astype(F32))
    early = exact(stack[...], images[...])
    early = jnp.concatenate([early, jnp.zeros((32, 80), F32)], axis=1)
    for i in range(16):
        early_send[i] = early[2 * i : 2 * i + 2]
    early1[q] = early_send[q]
    each_plane(lambda other, device: send(early_send.at[other], early1.at[q], 19, device))
    forward_partner(1)
    transposed_part(1)
    arrived(19, early1.at[pl.ds(0, 15)])
    acc = total(early1, 16)
    early2[zslot] = acc
    each_ring(lambda device: send(early2.at[zslot], early2.at[zslot], 20, device))
    forward_part(1)
    mine, theirs = column_sums(1)

    arrived(26, colp_recv.at[pl.ds(0, 15)])
    arrived(24, partner_p)
    pair = jnp.concatenate([unfold(mine), unfold(theirs)], axis=1)
    res_pair = jnp.concatenate([unfold(res_round.astype(F32)), unfold(colx[1, mate].astype(F32))], axis=1)
    p_pair = jnp.concatenate([pv[...], partner_p[...]], axis=1)
    hp_mine, hp_theirs = split(total(colp_recv, 16))
    hp_pair = jnp.concatenate([unfold(hp_mine), unfold(hp_theirs)], axis=1)
    late = exact(jnp.concatenate([res_pair, p_pair], axis=0), pair)
    late = late + exact(jnp.concatenate([pair, hp_pair], axis=0), res_pair)
    late = jnp.concatenate([late, jnp.zeros((16, 120), F32)], axis=1)
    late1[q] = jnp.sum(pltpu.roll(late, 0, 1, stride=8, stride_axis=0), axis=0, keepdims=True)
    each_plane(lambda other, device: send(late1.at[q], late1.at[q], 22, device))

    arrived(20, early2.at[pl.ds(0, 31)])
    early3[q] = total(early2, 32)
    each_plane(lambda other, device: send(early3.at[q], early3.at[q], 21, device))
    arrived(22, late1.at[pl.ds(0, 15)])
    late2[zslot] = total(late1, 16)
    each_ring(lambda device: send(late2.at[zslot], late2.at[zslot], 23, device))

    img_out[...] = unfold(finish(1, mine))
    cells = 1.0 / 131072.0
    place = jnp.where(
        lax.broadcasted_iota(jnp.int32, (128, 128), 0) == 8 + lax.rem(lax.broadcasted_iota(jnp.int32, (128, 128), 1), 8),
        1.0, 0.0,
    )
    arrived(21, early3.at[pl.ds(0, 15)])
    early = jnp.concatenate([early3[i] for i in range(16)], axis=0) * cells
    gs_out[...] = early[:24, :24]
    hx_part = pltpu.roll(early[:24], 128 - 32, 1)
    hp_part = pltpu.roll(early[:24], 128 - 8, 1)
    image_x = pltpu.roll(early[24:32], 128 - 32, 1)

    arrived(23, late2.at[pl.ds(0, 31)])
    late = total(late2, 32) * cells
    lane16 = lax.broadcasted_iota(jnp.int32, (16, 128), 1)
    late = jnp.where(lax.div(lane16, 8) == lax.broadcasted_iota(jnp.int32, (16, 128), 0), late, 0.0)
    late = exact(late, place)
    image_part = jnp.concatenate([image_x, late], axis=0)
    lane24 = lax.broadcasted_iota(jnp.int32, (24, 128), 1)
    whole = jnp.where(lane24 < 8, hx_part, jnp.where(lane24 < 16, image_part, hp_part))
    gh_out[...] = whole[:, :24]

    for which, ref in sent:
        wait_on(send_sem.at[which], ref)


def deliver(a, b, c, d, out_a, out_b, out_c, out_d, sem):
    pairs = ((a, out_a), (b, out_b), (c, out_c), (d, out_d))
    copies = [pltpu.make_async_copy(src, dst, sem.at[i]) for i, (src, dst) in enumerate(pairs)]
    for copy in copies:
        copy.start()
    for copy in copies:
        copy.wait()


def solution(mesh):
    def body(x_block, p_block, hp_block, tile_rows, tile_cols, tile_count, tile_values):
        any_spec = pl.BlockSpec(memory_space=pl.ANY)
        hbm = pl.BlockSpec(memory_space=pltpu.HBM)
        vmem = pl.BlockSpec(memory_space=pltpu.VMEM)
        shapes = (
            jax.ShapeDtypeStruct((8, 256), F32),
            jax.ShapeDtypeStruct((8, 256), F32),
            jax.ShapeDtypeStruct((24, 24), F32),
            jax.ShapeDtypeStruct((24, 24), F32),
        )
        results = pl.pallas_call(
            kernel,
            out_shape=shapes,
            in_specs=[any_spec] * 7,
            out_specs=(vmem,) * 4,
            scratch_shapes=[
                pltpu.VMEM((8, 256), F32), pltpu.VMEM((8, 256), F32), pltpu.VMEM((8, 256), F32),
                pltpu.VMEM((1, 1, SLOTS), jnp.int32), pltpu.VMEM((1, 1, SLOTS), jnp.int32),
                pltpu.SMEM((1, 1, SLOTS), jnp.int32), pltpu.SMEM((1, 1, SLOTS), jnp.int32),
                pltpu.SMEM((1, 1), jnp.int32),
                pltpu.VMEM((1, 1, SLOTS, 128, 128), BF16),
                pltpu.VMEM((256, SLOTS * 16), BF16), pltpu.VMEM((512, SLOTS * 16), BF16),
                pltpu.VMEM((SLOTS * 16, 128), BF16),
                pltpu.VMEM((2, 16, 16, 128), BF16), pltpu.VMEM((2, 32, 16, 128), BF16),
                pltpu.VMEM((2, 16, 16, 128), BF16), pltpu.VMEM((2, 16, 16, 128), BF16),
                pltpu.VMEM((2, 16, 32, 128), BF16), pltpu.VMEM((2, 16, 32, 128), BF16),
                pltpu.VMEM((2, 16, 128), F32), pltpu.VMEM((2, 16, 128), F32),
                pltpu.VMEM((32, 256), F32), pltpu.VMEM((48, 256), F32),
                pltpu.VMEM((8, 256), F32), pltpu.VMEM((8, 256), F32),
                pltpu.VMEM((16, 16, 128), BF16), pltpu.VMEM((16, 32, 128), BF16), pltpu.VMEM((16, 32, 128), BF16),
                pltpu.VMEM((16, 1, 128), F32), pltpu.VMEM((32, 1, 128), F32),
                pltpu.VMEM((16, 2, 128), F32), pltpu.VMEM((16, 2, 128), F32),
                pltpu.VMEM((32, 2, 128), F32), pltpu.VMEM((16, 2, 128), F32),
                pltpu.VMEM((16, 1, 128), F32), pltpu.VMEM((32, 1, 128), F32),
                pltpu.SemaphoreType.DMA((9,)), pltpu.SemaphoreType.DMA((27,)), pltpu.SemaphoreType.DMA((27,)),
            ],
            compiler_params=pltpu.CompilerParams(
                collective_id=0, has_side_effects=True, vmem_limit_bytes=VMEM_LIMIT
            ),
        )(x_block, p_block, hp_block, tile_rows, tile_cols, tile_count, tile_values)
        return pl.pallas_call(
            deliver,
            out_shape=shapes,
            in_specs=[any_spec] * 4,
            out_specs=(any_spec,) * 4,
            scratch_shapes=[pltpu.SemaphoreType.DMA((4,))],
        )(*results)

    in_specs = (
        P(None, ("row", "col")),
        P(None, ("row", "col")),
        P(None, ("row", "col")),
        P("row", "col", None),
        P("row", "col", None),
        P("row", "col"),
        P("row", "col", None, None, None),
    )
    out_specs = (P(None, ("row", "col")), P(None, ("row", "col")), P(), P())
    return jax.shard_map(body, mesh=mesh, in_specs=in_specs, out_specs=out_specs, check_vma=False)
```

time: 84.7 us -> 74.2 us (0.88)
  local copies, waits for them, and re-layouts: 7.2 us -> 0 us
  Pallas kernels: 75.9 us -> 72.7 us
    unnamed x16 -> x0, local copies, waits for them, and re-layouts: 7.2 us -> none
    pallas_call x1 -> x2, Pallas kernels: 75.9 us -> 72.7 us  [the longest x1 70.3 us: body(): pl.pallas_call(kernel, out_shape=shapes, in_specs=[any_spec] * 7, out_spe...]
where the time goes in v2:
time: 74.2 us; the launch traced here: 74 us
  Pallas kernels  72.7 us (98%)
  between operations  1.29 us (2%)
    pallas_call x1, Pallas kernels, body(): pl.pallas_call(kernel, out_shape=shapes, in_specs=[any_spec] * 7, out_spe...  70.3 us
    pallas_call x1, Pallas kernels, body(): pl.pallas_call(deliver, out_shape=shapes, in_specs=[any_spec] * 4, out_sp...  2.38 us

profile of v2, /device:TPU:1, one launch (start us, length us, event | category | flops | bytes accessed | tf_op | source)
XLA Modules:
  0.0 74.0 jit_solution(7837335145149689768)
XLA Ops:
  1.3 70.3 %shard_map.102 = (f32[8,256]{1,0:T(8,128)}, f32[8,256]{1,0:T(8,128)}, f32[24,24]{1,0:T(8,128)}, f32[24,24]{1,0:T(8,128)}) custom-call(f32[8,256]{1,0:T(8,128)} %x_hbm.1, f32[8,256]{1,0:T(8,128)} %p_hbm.1, f32[8,256]{1,0:T(8,128)} %hp_hbm.1, s32[1,1,48]{2,1,0:T(1,128)} %rows_hbm.1, s32[1,1,48]{2,1,0:T(1,128)} %cols_hbm.1, s32[1,1]{1,0:T(1,128)S(6)} %copy.11.count_hbm, ...), custom_call_target="tpu_custom_call" | custom-call | tf_op jit(solution)/shard_map/pallas_call | solution.py:363
  71.6 2.4 %shard_map.103 = (f32[8,256]{1,0:T(8,128)}, f32[8,256]{1,0:T(8,128)}, f32[24,24]{1,0:T(8,128)}, f32[24,24]{1,0:T(8,128)}) custom-call(f32[8,256]{1,0:T(8,128)} %get-tuple-element.8.a, f32[8,256]{1,0:T(8,128)} %get-tuple-element.9.b, f32[24,24]{1,0:T(8,128)} %get-tuple-element.10.c, f32[24,24]{1,0:T(8,128)} %get-tuple-element.11.d), custom_call_target="tpu_custom_call" | custom-call | tf_op jit(solution)/shard_map/pallas_call | solution.py:393

commit v3 on v2

--- a/solution.py
+++ b/solution.py
@@ -9,19 +9,20 @@
 F32 = jnp.float32
 BF16 = jnp.bfloat16
 SLOTS = 48
-UNROLL = 16
-VMEM_LIMIT = 60 * 1024 * 1024
+UNROLL = 48
+VMEM_LIMIT = 32 * 1024 * 1024
 NN = (((1,), (0,)), ((), ()))
 NT = (((1,), (1,)), ((), ()))
 def kernel(
     x_hbm, p_hbm, hp_hbm, rows_hbm, cols_hbm, count_hbm, tiles_hbm,
     res_out, img_out, gs_out, gh_out,
     xv, pv, hpv, rows_v, cols_v, rows_s, cols_s, count_s, tiles,
-    hot_f, hot_b, prod, rowx, colx, row_send, row_recv, col_send, col_recv,
+    hot_f, hot_b, prod, rowx0, rowx1, colx0, colx1, row_send, row_recv, col_send, col_recv,
     part_send, part_recv, stack, images, partner_x, partner_p, rowp, colp_send, colp_recv,
     th1, th2, early_send, early1, early2, early3, late1, late2,
     local_sem, send_sem, recv_sem,
 ):
+    rowx, colx = (rowx0, rowx1), (colx0, colx1)
     r = lax.axis_index("row")
     c = lax.axis_index("col")
     zh = lax.rem(r, 2)
@@ -113,10 +114,10 @@
     loads[0].wait()
     x_tall = fold(xv[...])
     x_round = x_tall.astype(BF16)
-    rowx[0, c] = x_round
+    rowx[0][c] = x_round
     loads[7].wait()
     rowp[c] = fold(pv[...]).astype(BF16)
-    colx[0, r] = x_round
+    colx[0][r] = x_round
 
     for i in (1, 2, 3):
         loads[i].wait()
@@ -157,14 +158,14 @@
 
     def send_gather(k):
         base = 8 * k
-        send(colx.at[k, r], colx.at[k, r], base + 1, partner)
-        each_line(lambda other, device: send(rowx.at[k, c], rowx.at[k, c], base, device))
-        each_plane(lambda other, device: send(colx.at[k, r], colx.at[k, r], base + 2, device))
+        each_line(lambda other, device: send(rowx[k].at[c], rowx[k].at[c], base, device))
+        send(colx[k].at[r], colx[k].at[r], base + 1, partner)
+        each_plane(lambda other, device: send(colx[k].at[r], colx[k].at[r], base + 2, device))
 
     def forward_partner(k):
         base = 8 * k
-        arrived(base + 1, colx.at[k, mate])
-        each_plane(lambda other, device: send(colx.at[k, mate], colx.at[k, mate], base + 3, device))
+        arrived(base + 1, colx[k].at[mate])
+        each_plane(lambda other, device: send(colx[k].at[mate], colx[k].at[mate], base + 3, device))
 
     def products(index, source, dims):
         def step(i, carry):
@@ -184,17 +185,17 @@
 
     def transposed_part(k):
         base = 8 * k
-        arrived(base, rowx.at[k, pl.ds(0, 15)])
-        products(rows_s, rowx.at[k], NN)
+        arrived(base, rowx[k].at[pl.ds(0, 15)])
+        products(rows_s, rowx[k], NN)
         to_columns(col_send.at[k])
         col_recv[k, q] = col_send[k, q]
         each_plane(lambda other, device: send(col_send.at[k, other], col_recv.at[k, q], base + 4, device))
 
     def forward_part(k):
         base = 8 * k
-        arrived(base + 2, colx.at[k, pl.ds(0, 15)])
-        arrived(base + 3, colx.at[k, pl.ds(0, 15)])
-        products(cols_s, colx.at[k], NT)
+        arrived(base + 2, colx[k].at[pl.ds(0, 15)])
+        arrived(base + 3, colx[k].at[pl.ds(0, 15)])
+        products(cols_s, colx[k], NT)
         for g in range(2):
             part = jnp.dot(hot_f[pl.ds(g * 128, 128), :], prod[...], preferred_element_type=F32)
             row_send[k, pl.ds(g * 8, 8)] = part.astype(BF16).reshape(8, 16, 128)
@@ -227,14 +228,13 @@
 
     send_gather(0)
     send(xv, partner_x, 16, partner)
-    send(pv, partner_p, 24, partner)
-    each_line(lambda other, device: send(rowp.at[c], rowp.at[c], 25, device))
     stack[0:8] = xv[...]
     stack[16:24] = pv[...]
     images[24:32] = hpv[...]
+    transposed_part(0)
     forward_partner(0)
-    transposed_part(0)
-    forward_part(0)
+    send(pv, partner_p, 24, partner)
+    each_line(lambda other, device: send(rowp.at[c], rowp.at[c], 25, device))
     mine, theirs = column_sums(0)
 
     arrived(16, partner_x)
@@ -247,6 +247,7 @@
     placed = jnp.where(lane8 == sub8, num, jnp.where(lane8 == sub8 + 8, den, 0.0))
     th1[q] = jnp.sum(placed, axis=0, keepdims=True)
     each_plane(lambda other, device: send(th1.at[q], th1.at[q], 17, device))
+    forward_part(0)
     arrived(17, th1.at[pl.ds(0, 15)])
     acc = total(th1, 16)
     th2[zslot] = acc
@@ -267,8 +268,8 @@
     theta_tall = jnp.concatenate([theta, theta], axis=0)
     res_tall = hx_tall - theta_tall * x_tall
     res_round = res_tall.astype(BF16)
-    rowx[1, c] = res_round
-    colx[1, r] = res_round
+    rowx[1][c] = res_round
+    colx[1][r] = res_round
 
     send_gather(1)
     residual = unfold(res_tall)
@@ -284,41 +285,44 @@
         early_send[i] = early[2 * i : 2 * i + 2]
     early1[q] = early_send[q]
     each_plane(lambda other, device: send(early_send.at[other], early1.at[q], 19, device))
+    transposed_part(1)
     forward_partner(1)
-    transposed_part(1)
     arrived(19, early1.at[pl.ds(0, 15)])
     acc = total(early1, 16)
     early2[zslot] = acc
     each_ring(lambda device: send(early2.at[zslot], early2.at[zslot], 20, device))
-    forward_part(1)
-    mine, theirs = column_sums(1)
 
     arrived(26, colp_recv.at[pl.ds(0, 15)])
     arrived(24, partner_p)
-    pair = jnp.concatenate([unfold(mine), unfold(theirs)], axis=1)
-    res_pair = jnp.concatenate([unfold(res_round.astype(F32)), unfold(colx[1, mate].astype(F32))], axis=1)
+    res_pair = jnp.concatenate([unfold(res_round.astype(F32)), unfold(colx[1][mate].astype(F32))], axis=1)
     p_pair = jnp.concatenate([pv[...], partner_p[...]], axis=1)
     hp_mine, hp_theirs = split(total(colp_recv, 16))
     hp_pair = jnp.concatenate([unfold(hp_mine), unfold(hp_theirs)], axis=1)
-    late = exact(jnp.concatenate([res_pair, p_pair], axis=0), pair)
-    late = late + exact(jnp.concatenate([pair, hp_pair], axis=0), res_pair)
+    other_side = jnp.concatenate([jnp.zeros((8, 8), F32), exact(hp_pair, res_pair)], axis=0)
+    sides = jnp.concatenate([res_pair, p_pair], axis=0)
+    mine, theirs = column_sums(1)
+    pair = jnp.concatenate([unfold(mine), unfold(theirs)], axis=1)
+    late = exact(sides, pair) + other_side
     late = jnp.concatenate([late, jnp.zeros((16, 120), F32)], axis=1)
     late1[q] = jnp.sum(pltpu.roll(late, 0, 1, stride=8, stride_axis=0), axis=0, keepdims=True)
     each_plane(lambda other, device: send(late1.at[q], late1.at[q], 22, device))
-
+    forward_part(1)
+
+    arrived(22, late1.at[pl.ds(0, 15)])
+    late2[zslot] = total(late1, 16)
+    each_ring(lambda device: send(late2.at[zslot], late2.at[zslot], 23, device))
     arrived(20, early2.at[pl.ds(0, 31)])
     early3[q] = total(early2, 32)
     each_plane(lambda other, device: send(early3.at[q], early3.at[q], 21, device))
-    arrived(22, late1.at[pl.ds(0, 15)])
-    late2[zslot] = total(late1, 16)
-    each_ring(lambda device: send(late2.at[zslot], late2.at[zslot], 23, device))
 
     img_out[...] = unfold(finish(1, mine))
     cells = 1.0 / 131072.0
-    place = jnp.where(
-        lax.broadcasted_iota(jnp.int32, (128, 128), 0) == 8 + lax.rem(lax.broadcasted_iota(jnp.int32, (128, 128), 1), 8),
-        1.0, 0.0,
-    )
+    from_lane = lax.broadcasted_iota(jnp.int32, (128, 256), 1)
+    from_vec = jnp.where(from_lane < 128, lax.rem(from_lane, 8), lax.div(from_lane - 128, 8))
+    place = jnp.where(lax.broadcasted_iota(jnp.int32, (128, 256), 0) == 8 + from_vec, 1.0, 0.0)
+    at = lax.broadcasted_iota(jnp.int32, (16, 256), 1)
+    at_row = lax.broadcasted_iota(jnp.int32, (16, 256), 0)
+    source = jnp.where(at < 128, lax.div(at, 8), jnp.where((at < 192) & (at_row < 8), lax.rem(at, 8), -1))
     arrived(21, early3.at[pl.ds(0, 15)])
     early = jnp.concatenate([early3[i] for i in range(16)], axis=0) * cells
     gs_out[...] = early[:24, :24]
@@ -328,9 +332,7 @@
 
     arrived(23, late2.at[pl.ds(0, 31)])
     late = total(late2, 32) * cells
-    lane16 = lax.broadcasted_iota(jnp.int32, (16, 128), 1)
-    late = jnp.where(lax.div(lane16, 8) == lax.broadcasted_iota(jnp.int32, (16, 128), 0), late, 0.0)
-    late = exact(late, place)
+    late = exact(jnp.where(source == at_row, jnp.concatenate([late, late], axis=1), 0.0), place)
     image_part = jnp.concatenate([image_x, late], axis=0)
     lane24 = lax.broadcasted_iota(jnp.int32, (24, 128), 1)
     whole = jnp.where(lane24 < 8, hx_part, jnp.where(lane24 < 16, image_part, hp_part))
@@ -373,7 +375,8 @@
                 pltpu.VMEM((1, 1, SLOTS, 128, 128), BF16),
                 pltpu.VMEM((256, SLOTS * 16), BF16), pltpu.VMEM((512, SLOTS * 16), BF16),
                 pltpu.VMEM((SLOTS * 16, 128), BF16),
-                pltpu.VMEM((2, 16, 16, 128), BF16), pltpu.VMEM((2, 32, 16, 128), BF16),
+                pltpu.VMEM((16, 16, 128), BF16), pltpu.VMEM((16, 16, 128), BF16),
+                pltpu.VMEM((32, 16, 128), BF16), pltpu.VMEM((32, 16, 128), BF16),
                 pltpu.VMEM((2, 16, 16, 128), BF16), pltpu.VMEM((2, 16, 16, 128), BF16),
                 pltpu.VMEM((2, 16, 32, 128), BF16), pltpu.VMEM((2, 16, 32, 128), BF16),
                 pltpu.VMEM((2, 16, 128), F32), pltpu.VMEM((2, 16, 128), F32),
@@ -389,14 +392,14 @@
             compiler_params=pltpu.CompilerParams(
                 collective_id=0, has_side_effects=True, vmem_limit_bytes=VMEM_LIMIT
             ),
-        )(x_block, p_block, hp_block, tile_rows, tile_cols, tile_count, tile_values)
+        )(*[pltpu.with_memory_space_constraint(v, pltpu.HBM) for v in (x_block, p_block, hp_block, tile_rows, tile_cols)], tile_count, pltpu.with_memory_space_constraint(tile_values, pltpu.HBM))
         return pl.pallas_call(
             deliver,
             out_shape=shapes,
             in_specs=[any_spec] * 4,
             out_specs=(any_spec,) * 4,
             scratch_shapes=[pltpu.SemaphoreType.DMA((4,))],
-        )(*results)
+        )(*[pltpu.with_memory_space_constraint(v, pltpu.VMEM) for v in results])
 
     in_specs = (
         P(None, ("row", "col")),

time: 74.2 us -> 68.4 us (0.922)
  Pallas kernels: 72.7 us -> 67 us
    pallas_call x1, Pallas kernels: 70.3 us -> 66.3 us  [body(): pl.pallas_call(kernel, out_shape=shapes, in_specs=[any_spec] * 7, out_spe...]
    pallas_call x1, Pallas kernels: 2.38 us -> 0.65 us  [body(): pl.pallas_call(deliver, out_shape=shapes, in_specs=[any_spec] * 4, out_sp...]
where the time goes in v3:
time: 68.4 us; the launch traced here: 68.3 us
  Pallas kernels  67 us (98%)
  between operations  1.29 us (2%)
    pallas_call x1, Pallas kernels, body(): pl.pallas_call(kernel, out_shape=shapes, in_specs=[any_spec] * 7, out_spe...  66.3 us

profile of v3, /device:TPU:1, one launch (start us, length us, event | category | flops | bytes accessed | tf_op | source)
XLA Modules:
  0.0 68.3 jit_solution(13300280571322483160)
XLA Ops:
  1.3 66.3 %shard_map.102 = (f32[8,256]{1,0:T(8,128)S(1)}, f32[8,256]{1,0:T(8,128)S(1)}, f32[24,24]{1,0:T(8,128)S(1)}, f32[24,24]{1,0:T(8,128)S(1)}) custom-call(f32[8,256]{1,0:T(8,128)} %x_hbm.1, f32[8,256]{1,0:T(8,128)} %p_hbm.1, f32[8,256]{1,0:T(8,128)} %hp_hbm.1, s32[1,1,48]{2,1,0:T(1,128)} %rows_hbm.1, s32[1,1,48]{2,1,0:T(1,128)} %cols_hbm.1, ...), custom_call_target="tpu_custom_call" | custom-call | tf_op jit(solution)/shard_map/pallas_call | solution.py:365
  67.6 0.7 shard_map.103

commit v4 on v3

--- a/solution.py
+++ b/solution.py
@@ -9,9 +9,7 @@
 F32 = jnp.float32
 BF16 = jnp.bfloat16
 SLOTS = 48
-UNROLL = 48
 VMEM_LIMIT = 32 * 1024 * 1024
-NN = (((1,), (0,)), ((), ()))
 NT = (((1,), (1,)), ((), ()))
 def kernel(
     x_hbm, p_hbm, hp_hbm, rows_hbm, cols_hbm, count_hbm, tiles_hbm,
@@ -32,7 +30,7 @@
     z = zh * 8 + lax.div(c, 2)
     mate = r + 1 - 2 * zh
     partner = (mate, c)
-    zslot = zh * 16 + c
+    spot = q * 2 + core
 
     def each_plane(act):
         def step(i, carry):
@@ -55,25 +53,34 @@
 
         lax.fori_loop(0, 15, step, 0)
 
-    def each_ring(act):
+    def each_pole(act):
+        def step(i, carry):
+            s = lax.div(i + 1, 2)
+            oz = lax.rem(z + 8 + jnp.where(lax.rem(i, 2) == 0, s, -s), 16)
+            act((q * 2 + lax.div(oz, 8), lax.rem(oz, 8) * 2 + core))
+            return carry
+
+        lax.fori_loop(0, 15, step, 0)
+
+    def each_disc(act):
         def step(i, carry):
             m = lax.div(i, 2)
-            s = lax.div(m + 1, 2)
-            d = 8 + jnp.where(lax.rem(m, 2) == 0, s, -s)
-            oz = lax.rem(z + d, 16)
+            a, b = lax.div(m, 4), lax.rem(m, 4)
+            dy = jnp.where(a < 2, 2 - a, 9 - 3 * a)
+            dx = jnp.where(b < 2, 2 - b, 9 - 3 * b)
+            other = lax.rem(y + dy, 4) * 4 + lax.rem(xx + dx, 4)
             k = jnp.where(m == 15, 1 - core, lax.rem(i, 2))
-            act((q * 2 + lax.div(oz, 8), lax.rem(oz, 8) * 2 + k))
+            act(other * 2 + k, (other * 2 + zh, c - core + k))
             return carry
 
         lax.fori_loop(0, 31, step, 0)
 
-    barrier = pltpu.get_barrier_semaphore()
-
-    def greet(device):
-        pl.semaphore_signal(barrier, inc=1, device_id=device, device_id_type=MESH)
-
-    each_ring(greet)
-    each_plane(lambda other, device: greet(device))
+    def each_far_pole(act):
+        def step(i, carry):
+            act((mate, 2 * i + core))
+            return carry
+
+        lax.fori_loop(0, 8, step, 0)
 
     loads = [
         pltpu.make_async_copy(src, dst, local_sem.at[i])
@@ -84,7 +91,17 @@
             ]
         )
     ]
-    for load in loads:
+    loads[0].start()
+    barrier = pltpu.get_barrier_semaphore()
+
+    def greet(device):
+        pl.semaphore_signal(barrier, inc=1, device_id=device, device_id_type=MESH)
+
+    each_far_pole(greet)
+    each_line(lambda other, device: greet(device))
+    each_disc(lambda other, device: greet(device))
+
+    for load in loads[1:]:
         load.start()
 
     def send(src, dst, which, device):
@@ -115,10 +132,98 @@
     x_tall = fold(xv[...])
     x_round = x_tall.astype(BF16)
     rowx[0][c] = x_round
-    loads[7].wait()
-    rowp[c] = fold(pv[...]).astype(BF16)
     colx[0][r] = x_round
 
+    pl.semaphore_wait(barrier, 54)
+
+    def send_gather(k):
+        base = 8 * k
+        each_line(lambda other, device: send(rowx[k].at[c], rowx[k].at[c], base, device))
+        send(colx[k].at[r], colx[k].at[r], base + 1, partner)
+        each_plane(lambda other, device: send(colx[k].at[r], colx[k].at[r], base + 2, device))
+
+    def forward_partner(k):
+        base = 8 * k
+        arrived(base + 1, colx[k].at[mate])
+        each_plane(lambda other, device: send(colx[k].at[mate], colx[k].at[mate], base + 3, device))
+
+    def products(index, source, dims):
+        for t in range(SLOTS):
+            block = source[lax.div(index[0, 0, t], 2)]
+            out = lax.dot_general(block, tiles[0, 0, t], dims, preferred_element_type=F32)
+            prod[16 * t : 16 * t + 16, :] = out.astype(BF16)
+
+    def paired_products(source):
+        none = jnp.zeros((16, 128), BF16)
+        for t in range(0, SLOTS, 2):
+            upper = jnp.concatenate([source[lax.div(rows_s[0, 0, t], 2)], none], axis=1)
+            lower = jnp.concatenate([none, source[lax.div(rows_s[0, 0, t + 1], 2)]], axis=1)
+            out = jnp.dot(
+                jnp.concatenate([upper, lower], axis=0),
+                tiles[0, 0, t : t + 2].reshape(256, 128),
+                preferred_element_type=F32,
+            )
+            prod[16 * t : 16 * t + 32, :] = out.astype(BF16)
+
+    def to_columns(out, landing, which):
+        for step in range(4):
+            g = lax.rem(y + (2, 1, 3, 0)[step], 4)
+            rows = pl.ds(pl.multiple_of(g * 128, 128), 128)
+            part = jnp.dot(hot_b[rows, :], prod[...], preferred_element_type=F32)
+            out[pl.ds(g * 4, 4)] = part.astype(BF16).reshape(4, 32, 128)
+            if step == 3:
+                landing[q] = out[q]
+
+            def give(i, carry):
+                other = g * 4 + lax.rem(xx + jnp.where(i < 2, 2 - i, 9 - 3 * i), 4)
+                send(out.at[other], landing.at[q], which, (other * 2 + zh, c))
+                return carry
+
+            lax.fori_loop(0, 3 if step == 3 else 4, give, 0)
+
+    def transposed_part(k):
+        base = 8 * k
+        arrived(base, rowx[k].at[pl.ds(0, 15)])
+        paired_products(rowx[k])
+        to_columns(col_send.at[k], col_recv.at[k], base + 4)
+
+    def forward_part(k):
+        base = 8 * k
+        arrived(base + 2, colx[k].at[pl.ds(0, 15)])
+        arrived(base + 3, colx[k].at[pl.ds(0, 15)])
+        products(cols_s, colx[k], NT)
+        for g in range(2):
+            part = jnp.dot(hot_f[pl.ds(g * 128, 128), :], prod[...], preferred_element_type=F32)
+            row_send[k, pl.ds(g * 8, 8)] = part.astype(BF16).reshape(8, 16, 128)
+        row_recv[k, c] = row_send[k, c]
+        each_line(lambda other, device: send(row_send.at[k, other], row_recv.at[k, c], base + 5, device))
+
+    def total(ref, n):
+        terms = [ref[i].astype(F32) for i in range(n)]
+        while len(terms) > 1:
+            terms = [a + b for a, b in zip(terms[::2], terms[1::2], strict=True)]
+        return terms[0]
+
+    def split(both):
+        return jnp.where(zh == 0, both[:16], both[16:]), jnp.where(zh == 0, both[16:], both[:16])
+
+    def column_sums(k):
+        base = 8 * k
+        arrived(base + 4, col_recv.at[k, pl.ds(0, 15)])
+        mine, theirs = split(total(col_recv.at[k], 16))
+        part_send[k] = theirs
+        send(part_send.at[k], part_recv.at[k], base + 6, partner)
+        return mine, theirs
+
+    def finish(k, mine):
+        base = 8 * k
+        arrived(base + 5, row_recv.at[k, pl.ds(0, 15)])
+        out = mine + total(row_recv.at[k], 16)
+        arrived(base + 6, part_recv.at[k])
+        return out + part_recv[k]
+
+    send_gather(0)
+    send(xv, partner_x, 16, partner)
     for i in (1, 2, 3):
         loads[i].wait()
     sub = lax.broadcasted_iota(jnp.int32, (16, SLOTS), 0)
@@ -154,80 +259,8 @@
     for i in (4, 5, 6, 8):
         loads[i].wait()
 
-    pl.semaphore_wait(barrier, 46)
-
-    def send_gather(k):
-        base = 8 * k
-        each_line(lambda other, device: send(rowx[k].at[c], rowx[k].at[c], base, device))
-        send(colx[k].at[r], colx[k].at[r], base + 1, partner)
-        each_plane(lambda other, device: send(colx[k].at[r], colx[k].at[r], base + 2, device))
-
-    def forward_partner(k):
-        base = 8 * k
-        arrived(base + 1, colx[k].at[mate])
-        each_plane(lambda other, device: send(colx[k].at[mate], colx[k].at[mate], base + 3, device))
-
-    def products(index, source, dims):
-        def step(i, carry):
-            for u in range(UNROLL):
-                t = i * UNROLL + u
-                block = source[lax.div(index[0, 0, t], 2)]
-                out = lax.dot_general(block, tiles[0, 0, t], dims, preferred_element_type=F32)
-                prod[pl.ds(pl.multiple_of(t * 16, 16), 16), :] = out.astype(BF16)
-            return carry
-
-        lax.fori_loop(0, SLOTS // UNROLL, step, 0)
-
-    def to_columns(out):
-        for g in range(4):
-            part = jnp.dot(hot_b[pl.ds(g * 128, 128), :], prod[...], preferred_element_type=F32)
-            out[pl.ds(g * 4, 4)] = part.astype(BF16).reshape(4, 32, 128)
-
-    def transposed_part(k):
-        base = 8 * k
-        arrived(base, rowx[k].at[pl.ds(0, 15)])
-        products(rows_s, rowx[k], NN)
-        to_columns(col_send.at[k])
-        col_recv[k, q] = col_send[k, q]
-        each_plane(lambda other, device: send(col_send.at[k, other], col_recv.at[k, q], base + 4, device))
-
-    def forward_part(k):
-        base = 8 * k
-        arrived(base + 2, colx[k].at[pl.ds(0, 15)])
-        arrived(base + 3, colx[k].at[pl.ds(0, 15)])
-        products(cols_s, colx[k], NT)
-        for g in range(2):
-            part = jnp.dot(hot_f[pl.ds(g * 128, 128), :], prod[...], preferred_element_type=F32)
-            row_send[k, pl.ds(g * 8, 8)] = part.astype(BF16).reshape(8, 16, 128)
-        row_recv[k, c] = row_send[k, c]
-        each_line(lambda other, device: send(row_send.at[k, other], row_recv.at[k, c], base + 5, device))
-
-    def total(ref, n):
-        out = ref[0].astype(F32)
-        for i in range(1, n):
-            out = out + ref[i].astype(F32)
-        return out
-
-    def split(both):
-        return jnp.where(zh == 0, both[:16], both[16:]), jnp.where(zh == 0, both[16:], both[:16])
-
-    def column_sums(k):
-        base = 8 * k
-        arrived(base + 4, col_recv.at[k, pl.ds(0, 15)])
-        mine, theirs = split(total(col_recv.at[k], 16))
-        part_send[k] = theirs
-        send(part_send.at[k], part_recv.at[k], base + 6, partner)
-        return mine, theirs
-
-    def finish(k, mine):
-        base = 8 * k
-        arrived(base + 5, row_recv.at[k, pl.ds(0, 15)])
-        out = mine + total(row_recv.at[k], 16)
-        arrived(base + 6, part_recv.at[k])
-        return out + part_recv[k]
-
-    send_gather(0)
-    send(xv, partner_x, 16, partner)
+    loads[7].wait()
+    rowp[c] = fold(pv[...]).astype(BF16)
     stack[0:8] = xv[...]
     stack[16:24] = pv[...]
     images[24:32] = hpv[...]
@@ -245,23 +278,21 @@
     sub8 = lax.broadcasted_iota(jnp.int32, (8, 128), 0)
     lane8 = lax.broadcasted_iota(jnp.int32, (8, 128), 1)
     placed = jnp.where(lane8 == sub8, num, jnp.where(lane8 == sub8 + 8, den, 0.0))
-    th1[q] = jnp.sum(placed, axis=0, keepdims=True)
-    each_plane(lambda other, device: send(th1.at[q], th1.at[q], 17, device))
+    th1[spot] = jnp.sum(placed, axis=0, keepdims=True)
+    each_disc(lambda other, device: send(th1.at[spot], th1.at[spot], 17, device))
     forward_part(0)
-    arrived(17, th1.at[pl.ds(0, 15)])
-    acc = total(th1, 16)
-    th2[zslot] = acc
-    each_ring(lambda device: send(th2.at[zslot], th2.at[zslot], 18, device))
+    arrived(17, th1.at[pl.ds(0, 31)])
+    acc = total(th1, 32)
+    th2[z] = acc
+    each_pole(lambda device: send(th2.at[z], th2.at[z], 18, device))
 
     arrived(25, rowp.at[pl.ds(0, 15)])
-    products(rows_s, rowp, NN)
-    to_columns(colp_send)
-    colp_recv[q] = colp_send[q]
-    each_plane(lambda other, device: send(colp_send.at[other], colp_recv.at[q], 26, device))
+    paired_products(rowp)
+    to_columns(colp_send, colp_recv, 26)
 
     hx_tall = finish(0, mine)
-    arrived(18, th2.at[pl.ds(0, 31)])
-    acc = total(th2, 32)
+    arrived(18, th2.at[pl.ds(0, 15)])
+    acc = total(th2, 16)
     num = 2.0 * jnp.sum(jnp.where(lane8 == sub8, acc, 0.0), axis=1, keepdims=True)
     den = jnp.sum(jnp.where(lane8 == sub8 + 8, acc, 0.0), axis=1, keepdims=True)
     theta = num / den
@@ -281,16 +312,16 @@
     images[40:48] = unfold(res_round.astype(F32))
     early = exact(stack[...], images[...])
     early = jnp.concatenate([early, jnp.zeros((32, 80), F32)], axis=1)
-    for i in range(16):
-        early_send[i] = early[2 * i : 2 * i + 2]
-    early1[q] = early_send[q]
-    each_plane(lambda other, device: send(early_send.at[other], early1.at[q], 19, device))
+    for i in range(32):
+        early_send[i] = early[i : i + 1]
+    early1[spot] = early_send[spot]
+    each_disc(lambda other, device: send(early_send.at[other], early1.at[spot], 19, device))
     transposed_part(1)
     forward_partner(1)
-    arrived(19, early1.at[pl.ds(0, 15)])
-    acc = total(early1, 16)
-    early2[zslot] = acc
-    each_ring(lambda device: send(early2.at[zslot], early2.at[zslot], 20, device))
+    arrived(19, early1.at[pl.ds(0, 31)])
+    acc = total(early1, 32)
+    early2[z] = acc
+    each_pole(lambda device: send(early2.at[z], early2.at[z], 20, device))
 
     arrived(26, colp_recv.at[pl.ds(0, 15)])
     arrived(24, partner_p)
@@ -299,21 +330,26 @@
     hp_mine, hp_theirs = split(total(colp_recv, 16))
     hp_pair = jnp.concatenate([unfold(hp_mine), unfold(hp_theirs)], axis=1)
     other_side = jnp.concatenate([jnp.zeros((8, 8), F32), exact(hp_pair, res_pair)], axis=0)
-    sides = jnp.concatenate([res_pair, p_pair], axis=0)
+    p_high = p_pair.astype(BF16).astype(F32)
+    sides = jnp.concatenate([res_pair, p_high, p_pair - p_high], axis=0).astype(BF16)
     mine, theirs = column_sums(1)
     pair = jnp.concatenate([unfold(mine), unfold(theirs)], axis=1)
-    late = exact(sides, pair) + other_side
+    high = pair.astype(BF16)
+    low = (pair - high.astype(F32)).astype(BF16)
+    late = lax.dot_general(sides, high, NT, preferred_element_type=F32)
+    late = late + lax.dot_general(sides, low, NT, preferred_element_type=F32)
+    late = late[0:16] + jnp.concatenate([jnp.zeros((8, 8), F32), late[16:24]], axis=0) + other_side
     late = jnp.concatenate([late, jnp.zeros((16, 120), F32)], axis=1)
-    late1[q] = jnp.sum(pltpu.roll(late, 0, 1, stride=8, stride_axis=0), axis=0, keepdims=True)
-    each_plane(lambda other, device: send(late1.at[q], late1.at[q], 22, device))
+    late1[spot] = jnp.sum(pltpu.roll(late, 0, 1, stride=8, stride_axis=0), axis=0, keepdims=True)
+    each_disc(lambda other, device: send(late1.at[spot], late1.at[spot], 22, device))
     forward_part(1)
 
-    arrived(22, late1.at[pl.ds(0, 15)])
-    late2[zslot] = total(late1, 16)
-    each_ring(lambda device: send(late2.at[zslot], late2.at[zslot], 23, device))
-    arrived(20, early2.at[pl.ds(0, 31)])
-    early3[q] = total(early2, 32)
-    each_plane(lambda other, device: send(early3.at[q], early3.at[q], 21, device))
+    arrived(22, late1.at[pl.ds(0, 31)])
+    late2[z] = total(late1, 32)
+    each_pole(lambda device: send(late2.at[z], late2.at[z], 23, device))
+    arrived(20, early2.at[pl.ds(0, 15)])
+    early3[spot] = total(early2, 16)
+    each_disc(lambda other, device: send(early3.at[spot], early3.at[spot], 21, device))
 
     img_out[...] = unfold(finish(1, mine))
     cells = 1.0 / 131072.0
@@ -323,16 +359,24 @@
     at = lax.broadcasted_iota(jnp.int32, (16, 256), 1)
     at_row = lax.broadcasted_iota(jnp.int32, (16, 256), 0)
     source = jnp.where(at < 128, lax.div(at, 8), jnp.where((at < 192) & (at_row < 8), lax.rem(at, 8), -1))
-    arrived(21, early3.at[pl.ds(0, 15)])
-    early = jnp.concatenate([early3[i] for i in range(16)], axis=0) * cells
+    arrived(21, early3.at[pl.ds(0, 31)])
+    early = jnp.concatenate([early3[i] for i in range(32)], axis=0) * cells
     gs_out[...] = early[:24, :24]
     hx_part = pltpu.roll(early[:24], 128 - 32, 1)
     hp_part = pltpu.roll(early[:24], 128 - 8, 1)
     image_x = pltpu.roll(early[24:32], 128 - 32, 1)
 
-    arrived(23, late2.at[pl.ds(0, 31)])
-    late = total(late2, 32) * cells
-    late = exact(jnp.where(source == at_row, jnp.concatenate([late, late], axis=1), 0.0), place)
+    arrived(23, late2.at[pl.ds(0, 15)])
+    late = total(late2, 16) * cells
+    parts, rest = [], late
+    for _ in range(3):
+        part = rest.astype(BF16).astype(F32)
+        rest = rest - part
+        parts.append(jnp.where(source == at_row, jnp.concatenate([part, part], axis=1), 0.0))
+    late = lax.dot_general(
+        jnp.concatenate(parts, axis=0).astype(BF16), place.astype(BF16), NT, preferred_element_type=F32
+    )
+    late = late[0:16] + late[16:32] + late[32:48]
     image_part = jnp.concatenate([image_x, late], axis=0)
     lane24 = lax.broadcasted_iota(jnp.int32, (24, 128), 1)
     whole = jnp.where(lane24 < 8, hx_part, jnp.where(lane24 < 16, image_part, hp_part))
@@ -383,10 +427,10 @@
                 pltpu.VMEM((32, 256), F32), pltpu.VMEM((48, 256), F32),
                 pltpu.VMEM((8, 256), F32), pltpu.VMEM((8, 256), F32),
                 pltpu.VMEM((16, 16, 128), BF16), pltpu.VMEM((16, 32, 128), BF16), pltpu.VMEM((16, 32, 128), BF16),
+                pltpu.VMEM((32, 1, 128), F32), pltpu.VMEM((16, 1, 128), F32),
+                pltpu.VMEM((32, 1, 128), F32), pltpu.VMEM((32, 1, 128), F32),
                 pltpu.VMEM((16, 1, 128), F32), pltpu.VMEM((32, 1, 128), F32),
-                pltpu.VMEM((16, 2, 128), F32), pltpu.VMEM((16, 2, 128), F32),
-                pltpu.VMEM((32, 2, 128), F32), pltpu.VMEM((16, 2, 128), F32),
-                pltpu.VMEM((16, 1, 128), F32), pltpu.VMEM((32, 1, 128), F32),
+                pltpu.VMEM((32, 1, 128), F32), pltpu.VMEM((16, 1, 128), F32),
                 pltpu.SemaphoreType.DMA((9,)), pltpu.SemaphoreType.DMA((27,)), pltpu.SemaphoreType.DMA((27,)),
             ],
             compiler_params=pltpu.CompilerParams(

time: 68.4 us -> 67.1 us (0.981)
  Pallas kernels: 67 us -> 65.6 us
    pallas_call x1, Pallas kernels: 66.3 us -> 65 us  [body(): pl.pallas_call(kernel, out_shape=shapes, in_specs=[any_spec] * 7, out_spe...]
where the time goes in v4:
time: 67.1 us; the launch traced here: 66.9 us
  Pallas kernels  65.6 us (98%)
  between operations  1.29 us (2%)
    pallas_call x1, Pallas kernels, body(): pl.pallas_call(kernel, out_shape=shapes, in_specs=[any_spec] * 7, out_spe...  65 us

profile of v4, /device:TPU:1, one launch (start us, length us, event | category | flops | bytes accessed | tf_op | source)
XLA Modules:
  0.0 66.9 jit_solution(4603308017419659524)
XLA Ops:
  1.3 65.0 %shard_map.102 = (f32[8,256]{1,0:T(8,128)S(1)}, f32[8,256]{1,0:T(8,128)S(1)}, f32[24,24]{1,0:T(8,128)S(1)}, f32[24,24]{1,0:T(8,128)S(1)}) custom-call(f32[8,256]{1,0:T(8,128)} %x_hbm.1, f32[8,256]{1,0:T(8,128)} %p_hbm.1, f32[8,256]{1,0:T(8,128)} %hp_hbm.1, s32[1,1,48]{2,1,0:T(1,128)} %rows_hbm.1, s32[1,1,48]{2,1,0:T(1,128)} %cols_hbm.1, ...), custom_call_target="tpu_custom_call" | custom-call | tf_op jit(solution)/shard_map/pallas_call | solution.py:409
  66.3 0.7 shard_map.103

commit v5 on v4

--- a/solution.py
+++ b/solution.py
@@ -51,7 +51,7 @@
             act(other, (r, other))
             return carry
 
-        lax.fori_loop(0, 15, step, 0)
+        lax.fori_loop(0, 15, step, 0, unroll=True)
 
     def each_pole(act):
         def step(i, carry):
@@ -60,7 +60,7 @@
             act((q * 2 + lax.div(oz, 8), lax.rem(oz, 8) * 2 + core))
             return carry
 
-        lax.fori_loop(0, 15, step, 0)
+        lax.fori_loop(0, 15, step, 0, unroll=True)
 
     def each_disc(act):
         def step(i, carry):
@@ -316,6 +316,14 @@
         early_send[i] = early[i : i + 1]
     early1[spot] = early_send[spot]
     each_disc(lambda other, device: send(early_send.at[other], early1.at[spot], 19, device))
+    arrived(26, colp_recv.at[pl.ds(0, 15)])
+    arrived(24, partner_p)
+    p_pair = jnp.concatenate([pv[...], partner_p[...]], axis=1)
+    p_high = p_pair.astype(BF16).astype(F32)
+    hp_mine, hp_theirs = split(total(colp_recv, 16))
+    hp_pair = jnp.concatenate([unfold(hp_mine), unfold(hp_theirs)], axis=1)
+    hp_high = hp_pair.astype(BF16)
+    hp_low = (hp_pair - hp_high.astype(F32)).astype(BF16)
     transposed_part(1)
     forward_partner(1)
     arrived(19, early1.at[pl.ds(0, 31)])
@@ -323,15 +331,17 @@
     early2[z] = acc
     each_pole(lambda device: send(early2.at[z], early2.at[z], 20, device))
 
-    arrived(26, colp_recv.at[pl.ds(0, 15)])
-    arrived(24, partner_p)
     res_pair = jnp.concatenate([unfold(res_round.astype(F32)), unfold(colx[1][mate].astype(F32))], axis=1)
-    p_pair = jnp.concatenate([pv[...], partner_p[...]], axis=1)
-    hp_mine, hp_theirs = split(total(colp_recv, 16))
-    hp_pair = jnp.concatenate([unfold(hp_mine), unfold(hp_theirs)], axis=1)
-    other_side = jnp.concatenate([jnp.zeros((8, 8), F32), exact(hp_pair, res_pair)], axis=0)
-    p_high = p_pair.astype(BF16).astype(F32)
-    sides = jnp.concatenate([res_pair, p_high, p_pair - p_high], axis=0).astype(BF16)
+    res_pair = res_pair.astype(BF16)
+    other_side = jnp.concatenate(
+        [
+            jnp.zeros((8, 8), F32),
+            lax.dot_general(hp_high, res_pair, NT, preferred_element_type=F32)
+            + lax.dot_general(hp_low, res_pair, NT, preferred_element_type=F32),
+        ],
+        axis=0,
+    )
+    sides = jnp.concatenate([res_pair.astype(F32), p_high, p_pair - p_high], axis=0).astype(BF16)
     mine, theirs = column_sums(1)
     pair = jnp.concatenate([unfold(mine), unfold(theirs)], axis=1)
     high = pair.astype(BF16)
@@ -366,6 +376,8 @@
     hp_part = pltpu.roll(early[:24], 128 - 8, 1)
     image_x = pltpu.roll(early[24:32], 128 - 32, 1)
 
+    for which, ref in sent:
+        wait_on(send_sem.at[which], ref)
     arrived(23, late2.at[pl.ds(0, 15)])
     late = total(late2, 16) * cells
     parts, rest = [], late
@@ -381,9 +393,7 @@
     lane24 = lax.broadcasted_iota(jnp.int32, (24, 128), 1)
     whole = jnp.where(lane24 < 8, hx_part, jnp.where(lane24 < 16, image_part, hp_part))
     gh_out[...] = whole[:, :24]
-
-    for which, ref in sent:
-        wait_on(send_sem.at[which], ref)
+    wait_on(send_sem.at[23], late2.at[pl.ds(0, 15)])
 
 
 def deliver(a, b, c, d, out_a, out_b, out_c, out_d, sem):

time: 67.1 us -> 67 us (level)
  no operation moved by 1% of the time
where the time goes in v5:
time: 67 us; the launch traced here: 66.9 us
  Pallas kernels  65.6 us (98%)
  between operations  1.29 us (2%)
    pallas_call x1, Pallas kernels, body(): pl.pallas_call(kernel, out_shape=shapes, in_specs=[any_spec] * 7, out_spe...  65 us

profile of v5, /device:TPU:1, one launch (start us, length us, event | category | flops | bytes accessed | tf_op | source)
XLA Modules:
  0.0 66.9 jit_solution(6660458330817478379)
XLA Ops:
  1.3 65.0 %shard_map.102 = (f32[8,256]{1,0:T(8,128)S(1)}, f32[8,256]{1,0:T(8,128)S(1)}, f32[24,24]{1,0:T(8,128)S(1)}, f32[24,24]{1,0:T(8,128)S(1)}) custom-call(f32[8,256]{1,0:T(8,128)} %x_hbm.1, f32[8,256]{1,0:T(8,128)} %p_hbm.1, f32[8,256]{1,0:T(8,128)} %hp_hbm.1, s32[1,1,48]{2,1,0:T(1,128)} %rows_hbm.1, s32[1,1,48]{2,1,0:T(1,128)} %cols_hbm.1, ...), custom_call_target="tpu_custom_call" | custom-call | tf_op jit(solution)/shard_map/pallas_call | solution.py:419
  66.3 0.7 shard_map.103
